TPU v7x, 256 devices: a whole 4x4x8 slice. The times are simulated.
256 devices in a mesh: src: 16 (over y_hi, x, core), dst: 16 (over y_lo, z).
Axes of the slice: x: 4, y: 4 (y_hi: 2, y_lo: 2; y = y_hi * 2 + y_lo), z: 8, core: 2. Of those that a mesh axis runs over, the one named last changes fastest.
Arguments:
- source_table: float32 [16384, 400], P(('src', 'dst')), may hold values from -1.5 to 1.5
- source_state: float32 [16384], P(('src', 'dst')), may hold values from 0.02 to 0.2
- target_table: float32 [16384, 400], P(('dst', 'src')), may hold values from -1.5 to 1.5
- target_state: float32 [16384], P(('dst', 'src')), may hold values from 0.02 to 0.2
- relations: bfloat16 [4, 400, 400], replicated, may hold values from -0.3125 to 0.3125
- edge_source: int32 [16, 16, 6144], P('src', 'dst'), may hold values from 0 to 1023
- edge_target: int32 [16, 16, 6144], P('src', 'dst'), may hold values from 0 to 1023
- batch_relation: int32 [16, 16, 12], P('src', 'dst'), may hold values from 0 to 3
- edge_counts: int32 [16, 16], P('src', 'dst'), may hold values from 768 to 6144, as said below
- negatives: int32 [16, 16, 12, 512], P('src', 'dst'), may hold values from 0 to 1023
Outputs:
- new_source_table: float32 [16384, 400], P(('src', 'dst'))
- new_source_state: float32 [16384], P(('src', 'dst'))
- new_target_table: float32 [16384, 400], P(('dst', 'src'))
- new_target_state: float32 [16384], P(('dst', 'src'))
Inputs may be any that keep to these rules, and one draw needn't show every extreme that they name: Only slots 0 to edge_counts[i, j] - 1 of a bucket are edges; some bucket holds 6144 in every draw.
All inputs are finite; a program needn't handle non-finite values.
Results may differ from a plain program's by a relative error of at most 0.0065.
Values may be sent and summed in bfloat16 or wider, within the bound.
No kernel may reach another device: no remote copies, remote signals or barrier semaphores. Data moves between devices by JAX's collectives and lax.ppermute only.
A program may use at most 64 MiB of HBM per device.

v0:
```python
import jax
import jax.numpy as jnp
from jax import lax
from jax.sharding import PartitionSpec as P

BATCH = 512
NEG = 512
BATCHES = 12


learn_rate = 0.5
epsilon = 1e-08


def make_queries(sources_all, source_ids, relation):
    rows_taken = sources_all[source_ids]
    return jnp.dot(rows_taken, relation, preferred_element_type=jnp.float32).astype(jnp.bfloat16)


def source_back(query_grad, relation):
    return lax.dot_general(
        query_grad.astype(jnp.bfloat16),
        relation,
        (((1,), (1,)), ((), ())),
        preferred_element_type=jnp.float32,
    )


def score_batch(queries, target_ids, negative_ids, weights, targets_all, target_acc):
    targets = targets_all[target_ids]
    negative_rows = targets_all[negative_ids]
    positive = jnp.sum(queries.astype(jnp.float32) * targets.astype(jnp.float32), axis=1)
    negative = lax.dot_general(
        queries, negative_rows, (((1,), (1,)), ((), ())), preferred_element_type=jnp.float32
    )
    pos_coef = -weights * jax.nn.sigmoid(-positive)
    neg_coef = (weights[:, None] * jax.nn.sigmoid(negative) / NEG).astype(jnp.bfloat16)
    query_grad = pos_coef[:, None] * targets.astype(jnp.float32) + jnp.dot(
        neg_coef, negative_rows, preferred_element_type=jnp.float32
    )
    target_term = pos_coef[:, None] * queries.astype(jnp.float32)
    negative_term = lax.dot_general(
        neg_coef, queries, (((0,), (0,)), ((), ())), preferred_element_type=jnp.float32
    )
    target_acc = target_acc.at[target_ids].add(target_term).at[negative_ids].add(negative_term)
    return (query_grad, target_acc)


def adagrad(table, state, grad):
    new_state = state + jnp.mean(grad * grad, axis=1)
    return (table - learn_rate * grad / (jnp.sqrt(new_state)[:, None] + epsilon), new_state)


def per_device(
    source_table,
    source_state,
    target_table,
    target_state,
    relations,
    edge_source,
    edge_target,
    batch_relation,
    edge_counts,
    negatives,
):
    sources_all = lax.all_gather(source_table.astype(jnp.bfloat16), "dst", axis=0, tiled=True)
    targets_all = lax.all_gather(target_table.astype(jnp.bfloat16), "src", axis=0, tiled=True)
    source_lists = edge_source[0, 0].reshape(BATCHES, BATCH)
    target_lists = edge_target[0, 0].reshape(BATCHES, BATCH)
    relation_list = batch_relation[0, 0]
    negative_lists = negatives[0, 0]
    valid_edges = edge_counts[0, 0]
    batch_total = (valid_edges + BATCH - 1) // BATCH
    offsets = jnp.arange(BATCH, dtype=jnp.int32)
    source_zero = jnp.zeros(sources_all.shape, jnp.float32)
    target_zero = jnp.zeros(targets_all.shape, jnp.float32)

    def edge_weights(position, limit):
        return (position * BATCH + offsets < limit).astype(jnp.float32)

    def full_batch(position, accums):
        source_acc, target_acc = accums
        relation = relations[relation_list[position]]
        queries = make_queries(sources_all, source_lists[position], relation)
        query_grad, target_acc = score_batch(
            queries,
            target_lists[position],
            negative_lists[position],
            edge_weights(position, valid_edges),
            targets_all,
            target_acc,
        )
        source_acc = source_acc.at[source_lists[position]].add(source_back(query_grad, relation))
        return (source_acc, target_acc)

    source_acc, target_acc = lax.fori_loop(0, batch_total, full_batch, (source_zero, target_zero))
    rows_owned = source_table.shape[0]
    source_whole = lax.psum(source_acc, "dst")
    source_grad = lax.dynamic_slice_in_dim(
        source_whole, lax.axis_index("dst") * rows_owned, rows_owned, 0
    )
    target_whole = lax.psum(target_acc, "src")
    target_grad = lax.dynamic_slice_in_dim(
        target_whole, lax.axis_index("src") * rows_owned, rows_owned, 0
    )
    new_source_table, new_source_state = adagrad(source_table, source_state, source_grad)
    new_target_table, new_target_state = adagrad(target_table, target_state, target_grad)
    return (new_source_table, new_source_state, new_target_table, new_target_state)


def solution(mesh):
    return jax.shard_map(
        per_device,
        mesh=mesh,
        in_specs=(
            P(("src", "dst"), None),
            P(("src", "dst")),
            P(("dst", "src"), None),
            P(("dst", "src")),
            P(),
            P("src", "dst", None),
            P("src", "dst", None),
            P("src", "dst", None),
            P("src", "dst"),
            P("src", "dst", None, None),
        ),
        out_specs=(
            P(("src", "dst"), None),
            P(("src", "dst")),
            P(("dst", "src"), None),
            P(("dst", "src")),
        ),
        check_vma=False,
    )
```

profile of v0, /device:TPU:2, one launch (start us, length us, event | category | flops | bytes accessed | tf_op | source)
XLA Modules:
  0.0 978.3 jit_solution(11473472460649887934)
XLA Ops:
  10.8 44.8 %all_gather.6 = bf16[1024,400]{1,0:T(8,128)(2,1)} all-gather(bf16[64,400]{1,0:T(8,128)(2,1)S(1)} %convert_element_type.33), channel_id=1, replica_groups=mesh['src'=16,'dst'=16] {'dst'}, dimensions={0}, use_global_device_ids=true | all-gather | bytes 870400 | tf_op jit(solution)/shard_map/all_gather | solution.py:66
  58.0 22.8 %all_gather.7 = bf16[1024,400]{1,0:T(8,128)(2,1)S(1)} all-gather(bf16[64,400]{1,0:T(8,128)(2,1)S(1)} %convert_element_type.34), channel_id=1, replica_groups=mesh['src'=16,'dst'=16] {'src'}, dimensions={0}, use_global_device_ids=true | all-gather | bytes 870400 | tf_op jit(solution)/shard_map/all_gather | solution.py:67
  82.7 302.1 %while.13 = (s32[]{:T(128)}, f32[1024,400]{1,0:T(8,128)}, f32[1024,400]{1,0:T(8,128)S(1)}, s32[]{:T(128)}, s32[12,512]{1,0:T(8,128)S(1)}, /*index=5*/s32[]{:T(12...) while((s32[]{:T(128)}, f32[1024,400]{1,0:T(8,128)}, ...), condition=%wide.region_5.6_spmd.clone, body=%wide.region_0.5_spmd.clone.sunk | while | flops 961277952 | bytes 21725952 | solution.py:96
  83.9 2.6 gather_fusion
  88.6 4.0 gather_fusion.1
  98.5 2.8 gather_fusion.2
  105.6 3.3 fusion.52
  109.0 7.1 scatter_fusion
  120.3 5.0 scatter_fusion.1
  127.9 5.0 scatter_fusion.2
  134.3 2.6 gather_fusion
  138.9 4.0 gather_fusion.1
  148.8 2.8 gather_fusion.2
  156.0 3.3 fusion.52
  159.3 7.1 scatter_fusion
  170.7 5.0 scatter_fusion.1
  175.7 2.6 fusion.53
  178.3 5.0 scatter_fusion.2
  184.6 2.6 gather_fusion
  189.3 4.0 gather_fusion.1
  199.2 2.8 gather_fusion.2
  206.3 3.3 fusion.52
  209.7 7.1 scatter_fusion
  221.0 5.0 scatter_fusion.1
  228.6 5.0 scatter_fusion.2
  235.0 2.6 gather_fusion
  239.6 4.0 gather_fusion.1
  249.5 2.8 gather_fusion.2
  256.7 3.3 fusion.52
  260.0 7.1 scatter_fusion
  271.4 5.0 scatter_fusion.1
  279.0 5.0 scatter_fusion.2
  285.3 2.6 gather_fusion
  290.0 4.0 gather_fusion.1
  299.8 2.8 gather_fusion.2
  307.0 3.3 fusion.52
  310.3 7.1 scatter_fusion
  321.7 5.0 scatter_fusion.1
  329.3 5.0 scatter_fusion.2
  335.7 2.6 gather_fusion
  340.3 4.0 gather_fusion.1
  350.2 2.8 gather_fusion.2
  357.3 3.3 fusion.52
  360.7 7.1 scatter_fusion
  372.0 5.0 scatter_fusion.1
  379.6 5.0 scatter_fusion.2
  386.1 436.3 %all-reduce.3.cloned.1.call-done = f32[1024,400]{1,0:T(8,128)} async-done(((f32[1024,400]{1,0:T(8,128)}), f32[1024,400]{1,0:T(8,128)}) %all-reduce.3.cloned.1.call-update) | async-done | bytes 1638416 | tf_op jit(solution)/shard_map/psum | solution.py:98
  823.9 142.7 %all-reduce.5.cloned.1.call-done = f32[1024,400]{1,0:T(8,128)} async-done(((f32[1024,400]{1,0:T(8,128)}), f32[1024,400]{1,0:T(8,128)}) %all-reduce.5.cloned.1.call-update) | async-done | bytes 1638416 | tf_op jit(solution)/shard_map/psum | solution.py:102
  (237 shorter events, 123.6 us)
Async XLA Ops:
  7.2 73.6 %copy-start.12 = (s32[1,1,12,512]{3,1,2,0:T(1,128)S(1)}, s32[1,1,12,512]{3,1,2,0:T(1,128)}, u32[]{:S(2)}) copy-start(s32[1,1,12,512]{3,1,2,0:T(1,128)} %param.21) | copy-start | bytes 73732
  7.2 815.2 %all-reduce.3.cloned.1.call-start = ((), (), s32[]{:S(2)}) async-start(), calls=%async_computation | async-start | bytes 4194304 | tf_op jit(solution)/shard_map/psum | solution.py:98
  82.7 11.6 %copy-start.8 = (s32[12,512]{1,0:T(8,128)}, s32[12,512]{1,0:T(8,128)S(1)}, u32[]{:S(2)}) copy-start(s32[12,512]{1,0:T(8,128)S(1)} %get-tuple-element.261) | copy-start | bytes 73732 | tf_op jit(solution)/shard_map/while
  82.7 11.6 %copy-start.10 = (s32[12,512]{1,0:T(8,128)}, s32[12,512]{1,0:T(8,128)S(1)}, u32[]{:S(2)}) copy-start(s32[12,512]{1,0:T(8,128)S(1)} %get-tuple-element.254) | copy-start | bytes 73732 | tf_op jit(solution)/shard_map/while
  82.7 5.8 copy-start.4
  127.9 5.1 copy-start.7
  127.9 5.1 copy-start.9
  127.9 5.1 copy-start.11
  127.9 5.1 copy-start.16
  133.0 11.6 %copy-start.8 = (s32[12,512]{1,0:T(8,128)}, s32[12,512]{1,0:T(8,128)S(1)}, u32[]{:S(2)}) copy-start(s32[12,512]{1,0:T(8,128)S(1)} %get-tuple-element.261) | copy-start | bytes 73732 | tf_op jit(solution)/shard_map/while
  133.0 11.6 %copy-start.10 = (s32[12,512]{1,0:T(8,128)}, s32[12,512]{1,0:T(8,128)S(1)}, u32[]{:S(2)}) copy-start(s32[12,512]{1,0:T(8,128)S(1)} %get-tuple-element.254) | copy-start | bytes 73732 | tf_op jit(solution)/shard_map/while
  133.1 5.8 copy-start.4
  178.3 5.1 copy-start.7
  178.3 5.1 copy-start.9
  178.3 5.1 copy-start.11
  178.3 5.1 copy-start.16
  183.4 11.6 %copy-start.8 = (s32[12,512]{1,0:T(8,128)}, s32[12,512]{1,0:T(8,128)S(1)}, u32[]{:S(2)}) copy-start(s32[12,512]{1,0:T(8,128)S(1)} %get-tuple-element.261) | copy-start | bytes 73732 | tf_op jit(solution)/shard_map/while
  183.4 11.6 %copy-start.10 = (s32[12,512]{1,0:T(8,128)}, s32[12,512]{1,0:T(8,128)S(1)}, u32[]{:S(2)}) copy-start(s32[12,512]{1,0:T(8,128)S(1)} %get-tuple-element.254) | copy-start | bytes 73732 | tf_op jit(solution)/shard_map/while
  183.4 5.8 copy-start.4
  228.6 5.1 copy-start.7
  228.6 5.1 copy-start.9
  228.6 5.1 copy-start.11
  228.6 5.1 copy-start.16
  233.7 11.6 %copy-start.8 = (s32[12,512]{1,0:T(8,128)}, s32[12,512]{1,0:T(8,128)S(1)}, u32[]{:S(2)}) copy-start(s32[12,512]{1,0:T(8,128)S(1)} %get-tuple-element.261) | copy-start | bytes 73732 | tf_op jit(solution)/shard_map/while
  233.7 11.6 %copy-start.10 = (s32[12,512]{1,0:T(8,128)}, s32[12,512]{1,0:T(8,128)S(1)}, u32[]{:S(2)}) copy-start(s32[12,512]{1,0:T(8,128)S(1)} %get-tuple-element.254) | copy-start | bytes 73732 | tf_op jit(solution)/shard_map/while
  233.8 5.8 copy-start.4
  278.9 5.1 copy-start.7
  278.9 5.1 copy-start.9
  278.9 5.1 copy-start.11
  279.0 5.1 copy-start.16
  284.1 11.6 %copy-start.8 = (s32[12,512]{1,0:T(8,128)}, s32[12,512]{1,0:T(8,128)S(1)}, u32[]{:S(2)}) copy-start(s32[12,512]{1,0:T(8,128)S(1)} %get-tuple-element.261) | copy-start | bytes 73732 | tf_op jit(solution)/shard_map/while
  284.1 11.6 %copy-start.10 = (s32[12,512]{1,0:T(8,128)}, s32[12,512]{1,0:T(8,128)S(1)}, u32[]{:S(2)}) copy-start(s32[12,512]{1,0:T(8,128)S(1)} %get-tuple-element.254) | copy-start | bytes 73732 | tf_op jit(solution)/shard_map/while
  284.1 5.8 copy-start.4
  329.3 5.1 copy-start.7
  329.3 5.1 copy-start.9
  329.3 5.1 copy-start.11
  329.3 5.1 copy-start.16
  334.4 11.6 %copy-start.8 = (s32[12,512]{1,0:T(8,128)}, s32[12,512]{1,0:T(8,128)S(1)}, u32[]{:S(2)}) copy-start(s32[12,512]{1,0:T(8,128)S(1)} %get-tuple-element.261) | copy-start | bytes 73732 | tf_op jit(solution)/shard_map/while
  334.4 11.6 %copy-start.10 = (s32[12,512]{1,0:T(8,128)}, s32[12,512]{1,0:T(8,128)S(1)}, u32[]{:S(2)}) copy-start(s32[12,512]{1,0:T(8,128)S(1)} %get-tuple-element.254) | copy-start | bytes 73732 | tf_op jit(solution)/shard_map/while
  334.5 5.8 copy-start.4
  379.6 5.1 copy-start.9
  379.6 5.1 copy-start.11
  379.6 5.1 copy-start.16
  384.7 438.7 %copy-start.13 = (f32[64]{0:T(128)S(1)}, f32[64]{0:T(128)}, u32[]{:S(2)}) copy-start(f32[64]{0:T(128)} %param.13) | copy-start | bytes 772
  384.7 582.9 %copy-start.14 = (f32[64]{0:T(128)S(1)}, f32[64]{0:T(128)}, u32[]{:S(2)}) copy-start(f32[64]{0:T(128)} %param.15) | copy-start | bytes 772
  384.8 583.4 %copy-start.1 = (f32[64,400]{1,0:T(8,128)S(1)}, f32[64,400]{1,0:T(8,128)}, u32[]{:S(2)}) copy-start(f32[64,400]{1,0:T(8,128)} %param.12) | copy-start | bytes 307204
  384.8 585.0 %copy-start.2 = (f32[64,400]{1,0:T(8,128)S(1)}, f32[64,400]{1,0:T(8,128)}, u32[]{:S(2)}) copy-start(f32[64,400]{1,0:T(8,128)} %param.14) | copy-start | bytes 307204
  384.8 581.8 %all-reduce.5.cloned.1.call-start = ((), (), s32[]{:S(2)}) async-start(), calls=%async_computation.1 | async-start | bytes 4194304 | tf_op jit(solution)/shard_map/psum | solution.py:102
  (21 other events, 30.8 us)
Sparse Core Ops, SparseCore 0:
  384.9 437.4 all-reduce.2
  825.0 141.5 all-reduce.4
where the time goes:
time: 990 us; the launch traced here: 978 us
  waiting for transfers between devices  579 us (58%)
  other arithmetic  147 us (15%)
  local copies, waits for them, and re-layouts  94.4 us (10%)
  blocking collectives  67.6 us (7%)
  matrix products  64.2 us (6%)
  between operations  14.8 us (1%)
  loops' own time  11.1 us (1%)
    psum x1, waiting for transfers between devices, per_device(): source_whole = lax.psum(source_acc, 'dst')  436 us
    psum x1, waiting for transfers between devices, per_device(): target_whole = lax.psum(target_acc, 'src')  143 us
    scatter-add x12, other arithmetic, score_batch(): target_acc.at[target_ids].add(target_term).at[negative_ids]  60.3 us
    all_gather x1, blocking collectives, per_device(): lax.all_gather(source_table.astype(jnp.bfloat16), 'dst', axis=0, tiled=True)  44.8 us
    scatter-add x6, other arithmetic, full_batch(): source_acc.at[source_lists[position]].add(source_back(query_grad, relation))  42.8 us
    gather x12, local copies, waits for them, and re-layouts, score_batch(): targets = targets_all[target_ids]  27.8 us
    gather x6, local copies, waits for them, and re-layouts, make_queries(): rows_taken = sources_all[source_ids]  24.1 us
    all_gather x1, blocking collectives, per_device(): lax.all_gather(target_table.astype(jnp.bfloat16), 'src', axis=0, tiled=True)  22.8 us
  transfers between devices with their start and end apart: 2, of which 2 were waited for; matrix products, arithmetic and copies ran while one was open for 0% of the time, Pallas kernels for 0%

commit v1 on v0

v1 whole, which is shorter than its diff:
```python
import functools

import jax
import jax.numpy as jnp
from jax import lax
from jax.experimental import pallas as pl
from jax.experimental.pallas import tpu as pltpu
from jax.sharding import PartitionSpec as P

BATCH = 512
NEG = 512
BATCHES = 12
NREL = 4
PART = 1024
DIM = 400
GROUP = 16
TILE = 256

learn_rate = 0.5
epsilon = 1e-08

NT = (((1,), (1,)), ((), ()))
TN = (((0,), (0,)), ((), ()))
VMEM_LIMIT = 56 * 1024 * 1024


def dot(a, b, dims=(((1,), (0,)), ((), ()))):
    return lax.dot_general(a, b, dims, preferred_element_type=jnp.float32)


def one_hot_columns(ids, rows, first, value):
    row = lax.broadcasted_iota(jnp.int32, (rows, ids.shape[1]), 0) + first
    return jnp.where(row == ids, jnp.float32(value), jnp.float32(0.0)).astype(jnp.bfloat16)


def histogram(ids, value):
    high = one_hot_columns(jnp.right_shift(ids, 7), 8, 0, 1.0)
    low = one_hot_columns(jnp.bitwise_and(ids, 127), 128, 0, value)
    table = dot(high, low, NT)
    return jnp.concatenate([table[k : k + 1] for k in range(8)], axis=1)


def count_kernel(rel_ref, cnt_ref, es_ref, et_ref, neg_ref, n_ref, m_ref, ohs, acc, srch, negh):
    step = pl.program_id(0)
    valid = cnt_ref[0]

    @pl.when(step == 0)
    def _():
        srch[...] = jnp.zeros_like(srch)
        negh[...] = jnp.zeros_like(negh)
        slot = lax.broadcasted_iota(jnp.int32, (1, BATCH), 1)
        batch_row = lax.broadcasted_iota(jnp.int32, (16, PART), 0)

        @pl.loop(0, BATCHES)
        def _(b):
            @pl.when(b * BATCH < valid)
            def _():
                at = pl.ds(pl.multiple_of(b * BATCH, BATCH), BATCH)
                ids = jnp.where(slot + b * BATCH < valid, es_ref[:, at], -1)
                ohs[b] = one_hot_columns(ids, PART, 0, 1.0)
                srch[...] = jnp.where(batch_row == b, histogram(ids, 1.0), srch[...])
                negh[...] = jnp.where(batch_row == b, histogram(neg_ref[:, at], 1.0 / 1024.0), negh[...])

    acc[...] = jnp.zeros_like(acc)

    @pl.loop(0, BATCHES)
    def _(b):
        @pl.when(b * BATCH < valid)
        def _():
            at = pl.ds(pl.multiple_of(b * BATCH, BATCH), BATCH)
            oht = one_hot_columns(et_ref[:, at], TILE, step * TILE, 0.5)
            r = rel_ref[b]
            acc[r] += dot(oht, ohs[b], NT)

    n_ref[...] = acc[...].astype(jnp.bfloat16)
    lanes = pl.ds(pl.multiple_of(step * TILE, TILE), TILE)
    negs = negh[:, lanes].astype(jnp.bfloat16)
    row = lax.broadcasted_iota(jnp.int32, (16, 1), 0)
    rel = jnp.full((16, 1), -1, jnp.int32)
    for b in range(BATCHES):
        rel = jnp.where(row == b, rel_ref[b], rel)
    for r in range(NREL):
        kept = jnp.where(rel == r, srch[...], 0.0).astype(jnp.bfloat16)
        m_ref[r] = dot(negs, kept, TN).astype(jnp.bfloat16)


def counts(rel, cnt, es, et, neg):
    smem = pl.BlockSpec(memory_space=pltpu.SMEM)
    whole = pl.BlockSpec((1, BATCHES * BATCH), lambda t: (0, 0))
    tiles = pl.BlockSpec((NREL, TILE, PART), lambda t: (0, t, 0))
    out = jax.ShapeDtypeStruct((NREL, PART, PART), jnp.bfloat16)
    return pl.pallas_call(
        count_kernel,
        grid=(PART // TILE,),
        in_specs=[smem, smem, whole, whole, whole],
        out_specs=[tiles, tiles],
        out_shape=[out, out],
        scratch_shapes=[
            pltpu.VMEM((BATCHES, PART, BATCH), jnp.bfloat16),
            pltpu.VMEM((NREL, TILE, PART), jnp.float32),
            pltpu.VMEM((16, PART), jnp.float32),
            pltpu.VMEM((16, PART), jnp.float32),
        ],
        compiler_params=pltpu.CompilerParams(vmem_limit_bytes=VMEM_LIMIT),
        cost_estimate=pl.CostEstimate(flops=2 * PART * PART * BATCHES * BATCH, bytes_accessed=16 << 20, transcendentals=0),
        name="pair_counts",
    )(rel, cnt, es, et, neg)


def score_kernel(s_ref, t_ref, rel_ref, n_ref, m_ref, gs_ref, gt_ref, q, tt, dqt, sacc, tacc):
    r, k = pl.program_id(0), pl.program_id(1)
    relation = rel_ref[0]

    @pl.when((r == 0) & (k == 0))
    def _():
        tt[...] = t_ref[...].astype(jnp.float32).T.astype(jnp.bfloat16)
        sacc[...] = jnp.zeros_like(sacc)
        tacc[...] = jnp.zeros_like(tacc)

    @pl.when(k == 0)
    def _():
        q[...] = dot(s_ref[...], relation).astype(jnp.bfloat16)
        dqt[...] = jnp.zeros_like(dqt)

    rows = pl.ds(pl.multiple_of(k * TILE, TILE), TILE)
    half = t_ref[rows] * jnp.bfloat16(0.5)
    th = jnp.tanh(dot(half, q[...], NT))
    coef = n_ref[0].astype(jnp.float32) * (th - 1.0) + m_ref[0].astype(jnp.float32) * (th + 1.0)
    coef = coef.astype(jnp.bfloat16)
    tacc[rows] += dot(coef, q[...])
    dqt[...] += dot(tt[:, rows], coef)

    @pl.when(k == pl.num_programs(1) - 1)
    def _():
        sacc[...] += dot(relation, dqt[...].astype(jnp.bfloat16))

    @pl.when((r == pl.num_programs(0) - 1) & (k == pl.num_programs(1) - 1))
    def _():
        gs_ref[...] = sacc[...].T.astype(jnp.bfloat16)
        gt_ref[...] = tacc[...].astype(jnp.bfloat16)


def gradients(sources, targets, relations, n, m):
    whole = pl.BlockSpec((PART, DIM), lambda r, k: (0, 0))
    tiles = pl.BlockSpec((1, TILE, PART), lambda r, k: (r, k, 0))
    out = jax.ShapeDtypeStruct((PART, DIM), jnp.bfloat16)
    return pl.pallas_call(
        score_kernel,
        grid=(NREL, PART // TILE),
        in_specs=[whole, whole, pl.BlockSpec((1, DIM, DIM), lambda r, k: (r, 0, 0)), tiles, tiles],
        out_specs=[whole, whole],
        out_shape=[out, out],
        scratch_shapes=[
            pltpu.VMEM((PART, DIM), jnp.bfloat16),
            pltpu.VMEM((DIM, PART), jnp.bfloat16),
            pltpu.VMEM((DIM, PART), jnp.float32),
            pltpu.VMEM((DIM, PART), jnp.float32),
            pltpu.VMEM((PART, DIM), jnp.float32),
        ],
        compiler_params=pltpu.CompilerParams(vmem_limit_bytes=VMEM_LIMIT),
        cost_estimate=pl.CostEstimate(flops=16 << 30, bytes_accessed=20 << 20, transcendentals=4 << 20),
        name="gradients",
    )(sources, targets, relations, n, m)


def update_kernel(part_ref, table_ref, state_ref, new_table_ref, new_state_ref):
    grad = part_ref[0].astype(jnp.float32)
    for k in range(1, GROUP):
        grad = grad + part_ref[k].astype(jnp.float32)
    rows = grad.shape[0]
    mean = jnp.sum(grad * grad, axis=1, keepdims=True) / DIM
    mean_row = jnp.broadcast_to(mean, (rows, 128)).T[:1]
    new_state_row = state_ref[...] + mean_row
    new_state_ref[...] = new_state_row
    new_state = jnp.broadcast_to(new_state_row, (128, rows)).T[:, :1]
    new_table_ref[...] = table_ref[...] - learn_rate * grad / (jnp.sqrt(new_state) + epsilon)


def update(parts, table, state):
    rows = table.shape[0]
    new_table, new_state = pl.pallas_call(
        update_kernel,
        out_shape=[jax.ShapeDtypeStruct(table.shape, jnp.float32), jax.ShapeDtypeStruct((1, rows), jnp.float32)],
        cost_estimate=pl.CostEstimate(flops=1 << 20, bytes_accessed=2 << 20, transcendentals=0),
        name="row_adagrad",
    )(parts, table, state.reshape(1, rows))
    return new_table, new_state.reshape(rows)


def spread(table, axis):
    rows = table.astype(jnp.bfloat16)
    blocks = jnp.broadcast_to(rows[None], (GROUP,) + rows.shape)
    return lax.all_to_all(blocks, axis, 0, 0).reshape(GROUP * rows.shape[0], rows.shape[1])


def per_device(
    source_table,
    source_state,
    target_table,
    target_state,
    relations,
    edge_source,
    edge_target,
    batch_relation,
    edge_counts,
    negatives,
):
    sources_all = spread(source_table, "dst")
    targets_all = spread(target_table, "src")
    slots = (1, BATCHES * BATCH)
    n, m = counts(
        batch_relation.reshape(BATCHES),
        edge_counts.reshape(1),
        edge_source.reshape(slots),
        edge_target.reshape(slots),
        negatives.reshape(slots),
    )
    source_grad, target_grad = gradients(sources_all, targets_all, relations, n, m)
    rows = source_table.shape[0]
    source_parts = lax.all_to_all(source_grad.reshape(GROUP, rows, DIM), "dst", 0, 0)
    target_parts = lax.all_to_all(target_grad.reshape(GROUP, rows, DIM), "src", 0, 0)
    new_source_table, new_source_state = update(source_parts, source_table, source_state)
    new_target_table, new_target_state = update(target_parts, target_table, target_state)
    return (new_source_table, new_source_state, new_target_table, new_target_state)


def solution(mesh):
    return jax.shard_map(
        per_device,
        mesh=mesh,
        in_specs=(
            P(("src", "dst"), None),
            P(("src", "dst")),
            P(("dst", "src"), None),
            P(("dst", "src")),
            P(),
            P("src", "dst", None),
            P("src", "dst", None),
            P("src", "dst", None),
            P("src", "dst"),
            P("src", "dst", None, None),
        ),
        out_specs=(
            P(("src", "dst"), None),
            P(("src", "dst")),
            P(("dst", "src"), None),
            P(("dst", "src")),
        ),
        check_vma=False,
    )
```

time: 990 us -> 161 us (0.16); the launches traced: 978 us -> 160 us
  waiting for transfers between devices: 579 us -> 48.8 us
  other arithmetic: 147 us -> 1.83 us
  local copies, waits for them, and re-layouts: 94.4 us -> 4.24 us
  matrix products: 64.2 us -> 0 us
  Pallas kernels: 0 us -> 50.1 us
  blocking collectives: 67.6 us -> 29.7 us
  starting transfers between devices: 0.08 us -> 23.6 us
  between operations: 14.8 us -> 1.31 us
  loops' own time: 11.1 us -> 0 us
    psum x2 -> x0, waiting for transfers between devices: 579 us -> none  [the longest x1 436 us: per_device(): source_whole = lax.psum(source_acc, 'dst')]
    scatter-add x18 -> x0, other arithmetic: 103 us -> none  [the longest x12 60.3 us: score_batch(): target_acc.at[target_ids].add(target_term).at[negative_ids]]
    gather x24 -> x0, local copies, waits for them, and re-layouts: 68.5 us -> none  [the longest x12 27.8 us: score_batch(): targets = targets_all[target_ids]]
    all_gather x2 -> x0, blocking collectives: 67.6 us -> none  [the longest x1 44.8 us: per_device(): lax.all_gather(source_table.astype(jnp.bfloat16), 'dst', axis=0, tiled=True)]
    dot_general x24 -> x0, matrix products: 64.2 us -> none  [the longest x6 20 us: source_back(): lax.dot_general(query_grad.astype(jnp.bfloat16), relation, (((1,), (1,)),...]
    pallas_call x0 -> x4, Pallas kernels: none -> 50.1 us  [the longest x1 27.2 us: gradients(): pl.pallas_call(score_kernel, grid=(NREL, PART // TILE), in_specs=[whole,...]
    all_to_all x0 -> x3, waiting for transfers between devices: none -> 48.8 us  [the longest x1 25.9 us: per_device(): lax.all_to_all(source_grad.reshape(GROUP, rows, DIM), 'dst', 0, 0)]
    all_to_all x0 -> x1, blocking collectives: none -> 29.7 us  [per_device(): lax.all_to_all(target_grad.reshape(GROUP, rows, DIM), 'src', 0, 0)]
  transfers between devices with their start and end apart: 2 -> 3, of which waited for: 2 -> 3; matrix products, arithmetic and copies ran while one was open for 0% -> 1% of each run, Pallas kernels for 0% -> 13%
where the time goes in v1:
time: 161 us; the launch traced here: 160 us
  Pallas kernels  50.1 us (31%)
  waiting for transfers between devices  48.8 us (30%)
  blocking collectives  29.7 us (18%)
  starting transfers between devices  23.6 us (15%)
  local copies, waits for them, and re-layouts  4.24 us (3%)
  other arithmetic  1.83 us (1%)
    all_to_all x1, blocking collectives, per_device(): lax.all_to_all(target_grad.reshape(GROUP, rows, DIM), 'src', 0, 0)  29.7 us
    pallas_call x1, Pallas kernels, gradients(): pl.pallas_call(score_kernel, grid=(NREL, PART // TILE), in_specs=[whole,...  27.2 us
    all_to_all x1, waiting for transfers between devices, per_device(): lax.all_to_all(source_grad.reshape(GROUP, rows, DIM), 'dst', 0, 0)  25.9 us
    all_to_all x2, waiting for transfers between devices, spread(): lax.all_to_all(blocks, axis, 0, 0)  22.9 us
    pallas_call x1, Pallas kernels, counts(): pl.pallas_call(count_kernel, grid=(PART // TILE,), in_specs=[smem, smem,...  18.1 us
    all_to_all x2, starting transfers between devices, spread(): lax.all_to_all(blocks, axis, 0, 0)  16.2 us
    all_to_all x1, starting transfers between devices, per_device(): lax.all_to_all(source_grad.reshape(GROUP, rows, DIM), 'dst', 0, 0)  7.39 us
    pallas_call x2, Pallas kernels, update(): pl.pallas_call(update_kernel, out_shape=[jax.ShapeDtypeStruct(table.shape...  4.81 us
  transfers between devices with their start and end apart: 3, of which 3 were waited for; matrix products, arithmetic and copies ran while one was open for 1% of the time, Pallas kernels for 13%

profile of v1, /device:TPU:2, one launch (start us, length us, event | category | flops | bytes accessed | tf_op | source)
XLA Modules:
  0.0 159.5 jit_solution(13145501421759205536)
XLA Ops:
  0.6 0.9 convert_element_type.7
  1.5 1.1 broadcast_in_dim.5
  2.6 7.5 %all-to-all-start.1 = ((bf16[16,64,400]{2,1,0:T(8,128)(2,1)}), bf16[16,64,400]{2,1,0:T(8,128)(2,1)S(1)}, u32[]{:S(2)}, u32[]{:S(2)}) async-start(bf16[16,64,400]{2,1,0:T(8,128)(2,1)} %broadcast_in_dim.5), calls=%async_computation.1 | async-start | bytes 2097152 | tf_op jit(solution)/shard_map/all_to_all | solution.py:193
  10.1 0.9 convert_element_type.6
  11.0 14.0 %all-to-all-done.1 = bf16[16,64,400]{2,1,0:T(8,128)(2,1)S(1)} async-done(((bf16[16,64,400]{2,1,0:T(8,128)(2,1)}), bf16[16,64,400]{2,1,0:T(8,128)(2,1)S(1)}, u32[]{:S(2)}, u32[]{:S(2)}) %all-to-all-start.1) | async-done | bytes 819232 | tf_op jit(solution)/shard_map/all_to_all | solution.py:193
  25.0 0.0 copy-start.1
  25.0 1.2 broadcast_in_dim.4
  26.2 8.7 %all-to-all-start = ((bf16[16,64,400]{2,1,0:T(8,128)(2,1)}), bf16[16,64,400]{2,1,0:T(8,128)(2,1)S(1)}, u32[]{:S(2)}, u32[]{:S(2)}) async-start(bf16[16,64,400]{2,1,0:T(8,128)(2,1)} %broadcast_in_dim.4), calls=%async_computation | async-start | bytes 2097152 | tf_op jit(solution)/shard_map/all_to_all | solution.py:193
  35.6 18.1 %pair_counts.1 = (bf16[4,1024,1024]{2,1,0:T(8,128)(2,1)}, bf16[4,1024,1024]{2,1,0:T(8,128)(2,1)}) custom-call(s32[12]{0:T(128)} %bitcast.23, s32[1]{0:T(128)} %bitcast.13.cnt_ref, s32[1,6144]{1,0:T(1,128)} %bitcast.20, s32[1,6144]{1,0:T(1,128)} %bitcast.21, s32[1,6144]{1,0:T(1,128)} %bitcast.22), custom_call_target="tpu_custom_call" | custom-call | flops 12884901888 | bytes 16777216 | tf_op jit(solution)/shard_map/pair_counts/pallas_call | solution.py:92
  53.6 0.0 copy-done.1
  53.6 8.9 %all-to-all-done = bf16[16,64,400]{2,1,0:T(8,128)(2,1)S(1)} async-done(((bf16[16,64,400]{2,1,0:T(8,128)(2,1)}), bf16[16,64,400]{2,1,0:T(8,128)(2,1)S(1)}, u32[]{:S(2)}, u32[]{:S(2)}) %all-to-all-start) | async-done | bytes 819232 | tf_op jit(solution)/shard_map/all_to_all | solution.py:193
  62.5 0.0 copy-start.2
  62.5 1.0 copy-done.2
  63.5 27.2 %gradients.1 = (bf16[1024,400]{1,0:T(8,128)(2,1)}, bf16[1024,400]{1,0:T(8,128)(2,1)}) custom-call(bf16[1024,400]{1,0:T(8,128)(2,1)} %bitcast.15, bf16[1024,400]{1,0:T(8,128)(2,1)} %bitcast.14, bf16[4,400,400]{2,1,0:T(8,128)(2,1)} %rel_ref.1, bf16[4,1024,1024]{2,1,0:T(8,128)(2,1)} %get-tuple-element.12.n_ref, bf16[4,1024,1024]{2,1,0:T(8,128)(2,1)} %get-tuple-element.13.m_ref), custom_call_target="tpu_custom_call" | custom-call | flops 17179869184 | bytes 20971520 | tf_op jit(solution)/shard_map/gradients/pallas_call | solution.py:147
  90.7 29.7 %all_to_all.20.part_ref = bf16[16,64,400]{2,1,0:T(8,128)(2,1)} all-to-all(bf16[16,64,400]{2,1,0:T(8,128)(2,1)} %bitcast.17), channel_id=1, replica_groups=mesh['src'=16,'dst'=16] {'src'}, dimensions={0} | all-to-all | bytes 1638400 | tf_op jit(solution)/shard_map/all_to_all | solution.py:221
  120.5 7.4 %all-to-all-start.2 = ((bf16[16,64,400]{2,1,0:T(8,128)(2,1)}), bf16[16,64,400]{2,1,0:T(8,128)(2,1)S(1)}, u32[]{:S(2)}, u32[]{:S(2)}) async-start(bf16[16,64,400]{2,1,0:T(8,128)(2,1)} %bitcast.16), calls=%async_computation.2 | async-start | bytes 2097152 | tf_op jit(solution)/shard_map/all_to_all | solution.py:220
  127.9 2.4 %row_adagrad.3 = (f32[64,400]{1,0:T(8,128)}, f32[1,64]{1,0:T(1,128)}) custom-call(bf16[16,64,400]{2,1,0:T(8,128)(2,1)} %all_to_all.20.part_ref, f32[64,400]{1,0:T(8,128)} %table_ref.3, f32[1,64]{1,0:T(1,128)} %bitcast.18), custom_call_target="tpu_custom_call" | custom-call | flops 1048576 | bytes 2097152 | tf_op jit(solution)/shard_map/row_adagrad/pallas_call | solution.py:181
  130.3 25.9 %all-to-all-done.2.part_ref = bf16[16,64,400]{2,1,0:T(8,128)(2,1)S(1)} async-done(((bf16[16,64,400]{2,1,0:T(8,128)(2,1)}), bf16[16,64,400]{2,1,0:T(8,128)(2,1)S(1)}, u32[]{:S(2)}, u32[]{:S(2)}) %all-to-all-start.2) | async-done | bytes 819232 | tf_op jit(solution)/shard_map/all_to_all | solution.py:220
  156.2 0.0 copy-start
  156.2 1.0 copy-done
  157.1 2.4 %row_adagrad.2 = (f32[64,400]{1,0:T(8,128)}, f32[1,64]{1,0:T(1,128)}) custom-call(bf16[16,64,400]{2,1,0:T(8,128)(2,1)} %copy-done, f32[64,400]{1,0:T(8,128)} %table_ref.2, f32[1,64]{1,0:T(1,128)} %bitcast.19), custom_call_target="tpu_custom_call" | custom-call | flops 1048576 | bytes 2097152 | tf_op jit(solution)/shard_map/row_adagrad/pallas_call | solution.py:181
Async XLA Ops:
  2.6 22.4 %all-to-all-start.1 = ((bf16[16,64,400]{2,1,0:T(8,128)(2,1)}), bf16[16,64,400]{2,1,0:T(8,128)(2,1)S(1)}, u32[]{:S(2)}, u32[]{:S(2)}) async-start(bf16[16,64,400]{2,1,0:T(8,128)(2,1)} %broadcast_in_dim.5), calls=%async_computation.1 | async-start | bytes 2097152 | tf_op jit(solution)/shard_map/all_to_all | solution.py:193
  25.0 28.6 %copy-start.1 = (bf16[16,64,400]{2,1,0:T(8,128)(2,1)}, bf16[16,64,400]{2,1,0:T(8,128)(2,1)S(1)}, u32[]{:S(2)}) copy-start(bf16[16,64,400]{2,1,0:T(8,128)(2,1)S(1)} %all-to-all-done.1) | copy-start | bytes 2457604
  26.2 36.3 %all-to-all-start = ((bf16[16,64,400]{2,1,0:T(8,128)(2,1)}), bf16[16,64,400]{2,1,0:T(8,128)(2,1)S(1)}, u32[]{:S(2)}, u32[]{:S(2)}) async-start(bf16[16,64,400]{2,1,0:T(8,128)(2,1)} %broadcast_in_dim.4), calls=%async_computation | async-start | bytes 2097152 | tf_op jit(solution)/shard_map/all_to_all | solution.py:193
  62.5 1.0 copy-start.2
  120.5 35.7 %all-to-all-start.2 = ((bf16[16,64,400]{2,1,0:T(8,128)(2,1)}), bf16[16,64,400]{2,1,0:T(8,128)(2,1)S(1)}, u32[]{:S(2)}, u32[]{:S(2)}) async-start(bf16[16,64,400]{2,1,0:T(8,128)(2,1)} %bitcast.16), calls=%async_computation.2 | async-start | bytes 2097152 | tf_op jit(solution)/shard_map/all_to_all | solution.py:220
  156.2 1.0 copy-start

commit v2 on v1

--- a/solution.py
+++ b/solution.py
@@ -1,5 +1,3 @@
-import functools
-
 import jax
 import jax.numpy as jnp
 from jax import lax
@@ -14,6 +12,7 @@
 PART = 1024
 DIM = 400
 GROUP = 16
+LINES = 208
 TILE = 256
 
 learn_rate = 0.5
@@ -107,27 +106,69 @@
     )(rel, cnt, es, et, neg)
 
 
-def score_kernel(s_ref, t_ref, rel_ref, n_ref, m_ref, gs_ref, gt_ref, q, tt, dqt, sacc, tacc):
+def pack(block):
+    parts = [block[:, 128 * c : 128 * c + 128] for c in range(3)]
+    tail = [block[16 * g : 16 * g + 16, 384:DIM] for g in range(4)]
+    parts.append(jnp.concatenate(tail + [jnp.zeros((16, 64), block.dtype)], axis=1))
+    return jnp.concatenate(parts, axis=0)
+
+
+def unpack(lines):
+    parts = [lines[64 * c : 64 * c + 64] for c in range(3)]
+    tail = [lines[192:208, 16 * g : 16 * g + 16] for g in range(4)]
+    parts.append(jnp.concatenate(tail, axis=0))
+    return jnp.concatenate(parts, axis=1)
+
+
+def pack_kernel(source_ref, target_ref, spread_ref, packed_ref):
+    lines = pack(source_ref[...]).astype(jnp.bfloat16)
+    for d in range(GROUP):
+        spread_ref[d] = lines
+    packed_ref[...] = pack(target_ref[...]).astype(jnp.bfloat16)
+
+
+def pack_tables(source_table, target_table):
+    return pl.pallas_call(
+        pack_kernel,
+        out_shape=[
+            jax.ShapeDtypeStruct((GROUP, LINES, 128), jnp.bfloat16),
+            jax.ShapeDtypeStruct((LINES, 128), jnp.bfloat16),
+        ],
+        name="pack_tables",
+    )(source_table, target_table)
+
+
+def place(member, near, other):
+    high, x, core = member // 8, (member // 2) % 4, member % 2
+    return jnp.bitwise_xor(high, near % 2) * 8 + ((x + 4 - near // 2) % 4) * 2 + jnp.bitwise_xor(core, other)
+
+
+def score_kernel(member_ref, s_ref, t_own_ref, t_other_ref, rel_ref, n_ref, m_ref, gs_ref, a_ref, q_ref, s, t, tt, dqt, sacc):
     r, k = pl.program_id(0), pl.program_id(1)
     relation = rel_ref[0]
 
     @pl.when((r == 0) & (k == 0))
     def _():
-        tt[...] = t_ref[...].astype(jnp.float32).T.astype(jnp.bfloat16)
+        for d in range(GROUP):
+            s[64 * d : 64 * d + 64] = unpack(s_ref[d])
+        for other, ref in enumerate((t_own_ref, t_other_ref)):
+            for near in range(8):
+                first = pl.multiple_of(place(member_ref[0], near, other) * 64, 64)
+                t[pl.ds(first, 64)] = unpack(ref[near])
+        tt[...] = t[...].astype(jnp.float32).T.astype(jnp.bfloat16)
         sacc[...] = jnp.zeros_like(sacc)
-        tacc[...] = jnp.zeros_like(tacc)
 
     @pl.when(k == 0)
     def _():
-        q[...] = dot(s_ref[...], relation).astype(jnp.bfloat16)
+        q_ref[0] = dot(s[...], relation).astype(jnp.bfloat16)
         dqt[...] = jnp.zeros_like(dqt)
 
     rows = pl.ds(pl.multiple_of(k * TILE, TILE), TILE)
-    half = t_ref[rows] * jnp.bfloat16(0.5)
-    th = jnp.tanh(dot(half, q[...], NT))
+    half = t[rows] * jnp.bfloat16(0.5)
+    th = jnp.tanh(dot(half, q_ref[0], NT))
     coef = n_ref[0].astype(jnp.float32) * (th - 1.0) + m_ref[0].astype(jnp.float32) * (th + 1.0)
     coef = coef.astype(jnp.bfloat16)
-    tacc[rows] += dot(coef, q[...])
+    a_ref[0] = coef
     dqt[...] += dot(tt[:, rows], coef)
 
     @pl.when(k == pl.num_programs(1) - 1)
@@ -136,37 +177,92 @@
 
     @pl.when((r == pl.num_programs(0) - 1) & (k == pl.num_programs(1) - 1))
     def _():
-        gs_ref[...] = sacc[...].T.astype(jnp.bfloat16)
-        gt_ref[...] = tacc[...].astype(jnp.bfloat16)
-
-
-def gradients(sources, targets, relations, n, m):
-    whole = pl.BlockSpec((PART, DIM), lambda r, k: (0, 0))
+        for d in range(0, GROUP, 2):
+            pair = sacc[:, 64 * d : 64 * d + 128].T.astype(jnp.bfloat16)
+            gs_ref[d] = pack(pair[:64])
+            gs_ref[d + 1] = pack(pair[64:])
+
+
+def source_gradients(member, sources, targets_own, targets_other, relations, n, m):
     tiles = pl.BlockSpec((1, TILE, PART), lambda r, k: (r, k, 0))
-    out = jax.ShapeDtypeStruct((PART, DIM), jnp.bfloat16)
+    blocks = lambda count: pl.BlockSpec((count, LINES, 128), lambda r, k: (0, 0, 0))
     return pl.pallas_call(
         score_kernel,
         grid=(NREL, PART // TILE),
-        in_specs=[whole, whole, pl.BlockSpec((1, DIM, DIM), lambda r, k: (r, 0, 0)), tiles, tiles],
-        out_specs=[whole, whole],
-        out_shape=[out, out],
+        in_specs=[
+            pl.BlockSpec(memory_space=pltpu.SMEM),
+            blocks(GROUP),
+            blocks(8),
+            blocks(8),
+            pl.BlockSpec((1, DIM, DIM), lambda r, k: (r, 0, 0)),
+            tiles,
+            tiles,
+        ],
+        out_specs=[blocks(GROUP), tiles, pl.BlockSpec((1, PART, DIM), lambda r, k: (r, 0, 0))],
+        out_shape=[
+            jax.ShapeDtypeStruct((GROUP, LINES, 128), jnp.bfloat16),
+            jax.ShapeDtypeStruct((NREL, PART, PART), jnp.bfloat16),
+            jax.ShapeDtypeStruct((NREL, PART, DIM), jnp.bfloat16),
+        ],
         scratch_shapes=[
+            pltpu.VMEM((PART, DIM), jnp.bfloat16),
             pltpu.VMEM((PART, DIM), jnp.bfloat16),
             pltpu.VMEM((DIM, PART), jnp.bfloat16),
             pltpu.VMEM((DIM, PART), jnp.float32),
             pltpu.VMEM((DIM, PART), jnp.float32),
-            pltpu.VMEM((PART, DIM), jnp.float32),
         ],
         compiler_params=pltpu.CompilerParams(vmem_limit_bytes=VMEM_LIMIT),
-        cost_estimate=pl.CostEstimate(flops=16 << 30, bytes_accessed=20 << 20, transcendentals=4 << 20),
-        name="gradients",
-    )(sources, targets, relations, n, m)
+        cost_estimate=pl.CostEstimate(flops=12 << 30, bytes_accessed=32 << 20, transcendentals=4 << 20),
+        name="source_gradients",
+    )(member, sources, targets_own, targets_other, relations, n, m)
+
+
+def target_kernel(member_ref, a_ref, q_ref, own_ref, other_ref):
+    step = pl.program_id(0)
+    member = member_ref[0]
+    high, x, core = member // 8, (member // 2) % 4, member % 2
+    grad = dot(a_ref[0], q_ref[0])
+    for r in range(1, NREL):
+        grad = grad + dot(a_ref[r], q_ref[r])
+    grad = grad.astype(jnp.bfloat16)
+    for u in range(4):
+        at = step * 4 + u
+        near = (((at // 2) % 4 + 4 - x) % 4) * 2 + jnp.bitwise_xor(at // 8, high)
+        lines = pack(grad[64 * u : 64 * u + 64])
+
+        @pl.when(core == u % 2)
+        def _():
+            own_ref[near] = lines
+
+        @pl.when(core != u % 2)
+        def _():
+            other_ref[near] = lines
+
+
+def target_gradients(member, a, q):
+    out = jax.ShapeDtypeStruct((8, LINES, 128), jnp.bfloat16)
+    whole = pl.BlockSpec((8, LINES, 128), lambda k: (0, 0, 0))
+    return pl.pallas_call(
+        target_kernel,
+        grid=(PART // TILE,),
+        in_specs=[
+            pl.BlockSpec(memory_space=pltpu.SMEM),
+            pl.BlockSpec((NREL, TILE, PART), lambda k: (0, k, 0)),
+            pl.BlockSpec((NREL, PART, DIM), lambda k: (0, 0, 0)),
+        ],
+        out_specs=[whole, whole],
+        out_shape=[out, out],
+        compiler_params=pltpu.CompilerParams(vmem_limit_bytes=VMEM_LIMIT),
+        cost_estimate=pl.CostEstimate(flops=4 << 30, bytes_accessed=12 << 20, transcendentals=0),
+        name="target_gradients",
+    )(member, a, q)
 
 
 def update_kernel(part_ref, table_ref, state_ref, new_table_ref, new_state_ref):
-    grad = part_ref[0].astype(jnp.float32)
-    for k in range(1, GROUP):
-        grad = grad + part_ref[k].astype(jnp.float32)
+    lines = part_ref[0].astype(jnp.float32)
+    for k in range(1, part_ref.shape[0]):
+        lines = lines + part_ref[k].astype(jnp.float32)
+    grad = unpack(lines)
     rows = grad.shape[0]
     mean = jnp.sum(grad * grad, axis=1, keepdims=True) / DIM
     mean_row = jnp.broadcast_to(mean, (rows, 128)).T[:1]
@@ -187,10 +283,28 @@
     return new_table, new_state.reshape(rows)
 
 
-def spread(table, axis):
-    rows = table.astype(jnp.bfloat16)
-    blocks = jnp.broadcast_to(rows[None], (GROUP,) + rows.shape)
-    return lax.all_to_all(blocks, axis, 0, 0).reshape(GROUP * rows.shape[0], rows.shape[1])
+HALVES = [(i, i ^ 8) for i in range(16)]
+CORES = [(i, i ^ 1) for i in range(16)]
+
+
+def x_step(k):
+    return [(i, (i & 9) | ((((i >> 1) + k) & 3) << 1)) for i in range(16)]
+
+
+def gather_src(lines):
+    near = jnp.stack([lines, lax.ppermute(lines, "src", HALVES)])
+    own = jnp.concatenate([near] + [lax.ppermute(near, "src", x_step(k)) for k in (1, 2, 3)])
+    return own, lax.ppermute(own, "src", CORES)
+
+
+def scatter_src(own, other):
+    total = own.astype(jnp.float32) + lax.ppermute(other, "src", CORES).astype(jnp.float32)
+    sent = total.astype(jnp.bfloat16)
+    here = total[:2]
+    for k in (1, 2, 3):
+        here = here + lax.ppermute(sent[2 * k : 2 * k + 2], "src", x_step(k)).astype(jnp.float32)
+    far = lax.ppermute(here[1].astype(jnp.bfloat16), "src", HALVES)
+    return jnp.stack([here[0], far.astype(jnp.float32)])
 
 
 def per_device(
@@ -205,8 +319,10 @@
     edge_counts,
     negatives,
 ):
-    sources_all = spread(source_table, "dst")
-    targets_all = spread(target_table, "src")
+    member = lax.axis_index("src").reshape(1)
+    source_blocks, target_lines = pack_tables(source_table, target_table)
+    sources_all = lax.all_to_all(source_blocks, "dst", 0, 0)
+    targets_own, targets_other = gather_src(target_lines)
     slots = (1, BATCHES * BATCH)
     n, m = counts(
         batch_relation.reshape(BATCHES),
@@ -215,10 +331,9 @@
         edge_target.reshape(slots),
         negatives.reshape(slots),
     )
-    source_grad, target_grad = gradients(sources_all, targets_all, relations, n, m)
-    rows = source_table.shape[0]
-    source_parts = lax.all_to_all(source_grad.reshape(GROUP, rows, DIM), "dst", 0, 0)
-    target_parts = lax.all_to_all(target_grad.reshape(GROUP, rows, DIM), "src", 0, 0)
+    source_grad, a, q = source_gradients(member, sources_all, targets_own, targets_other, relations, n, m)
+    source_parts = lax.all_to_all(source_grad, "dst", 0, 0)
+    target_parts = scatter_src(*target_gradients(member, a, q))
     new_source_table, new_source_state = update(source_parts, source_table, source_state)
     new_target_table, new_target_state = update(target_parts, target_table, target_state)
     return (new_source_table, new_source_state, new_target_table, new_target_state)

time: 161 us -> 140 us (0.87)
  starting transfers between devices: 23.6 us -> 54.8 us
  blocking collectives: 29.7 us -> 0 us
  waiting for transfers between devices: 48.8 us -> 20.5 us
  Pallas kernels: 50.1 us -> 56.7 us
    all_to_all x3 -> x2, waiting for transfers between devices: 48.8 us -> 4.49 us  [the longest x1 4.49 us: per_device(): source_parts = lax.all_to_all(source_grad, 'dst', 0, 0)]
    all_to_all x1 -> x0, blocking collectives: 29.7 us -> none  [per_device(): lax.all_to_all(target_grad.reshape(GROUP, rows, DIM), 'src', 0, 0)]
    ppermute x0 -> x10, waiting for transfers between devices: none -> 16 us  [the longest x3 5.81 us: scatter_src(): lax.ppermute(sent[2 * k:2 * k + 2], 'src', x_step(k)).astype(jnp.float32)]
    all_to_all x3 -> x2, starting transfers between devices: 23.6 us -> 39.2 us  [the longest x1 29.6 us: per_device(): source_parts = lax.all_to_all(source_grad, 'dst', 0, 0)]
    ppermute x0 -> x10, starting transfers between devices: none -> 15.6 us  [the longest x3 4.83 us: gather_src(): lax.ppermute(near, 'src', x_step(k))]
    pallas_call x1 -> x3, Pallas kernels: 27.2 us -> 39.2 us  [the longest x1 27.2 us: source_gradients(): pl.pallas_call(score_kernel, grid=(NREL, PART // TILE), in_specs=[pl.Bloc...]
    pallas_call x1, Pallas kernels: 18.1 us -> 13.1 us  [counts(): pl.pallas_call(count_kernel, grid=(PART // TILE,), in_specs=[smem, smem,...]
    broadcast_in_dim x2 -> x0, local copies, waits for them, and re-layouts: 2.26 us -> none  [spread(): blocks = jnp.broadcast_to(rows[None], (GROUP,) + rows.shape)]
  transfers between devices with their start and end apart: 3 -> 12, of which waited for: 3 -> 6; matrix products, arithmetic and copies ran while one was open for 1% -> 3% of each run, Pallas kernels for 13% -> 11%
where the time goes in v2:
time: 140 us; the launch traced here: 139 us
  Pallas kernels  56.7 us (40%)
  starting transfers between devices  54.8 us (39%)
  waiting for transfers between devices  20.5 us (15%)
  local copies, waits for them, and re-layouts  2.91 us (2%)
  other arithmetic  2.71 us (2%)
  between operations  1.43 us (1%)
    all_to_all x1, starting transfers between devices, per_device(): source_parts = lax.all_to_all(source_grad, 'dst', 0, 0)  29.6 us
    pallas_call x1, Pallas kernels, source_gradients(): pl.pallas_call(score_kernel, grid=(NREL, PART // TILE), in_specs=[pl.Bloc...  27.2 us
    pallas_call x1, Pallas kernels, counts(): pl.pallas_call(count_kernel, grid=(PART // TILE,), in_specs=[smem, smem,...  13.1 us
    pallas_call x1, Pallas kernels, target_gradients(): pl.pallas_call(target_kernel, grid=(PART // TILE,), in_specs=[pl.BlockSpe...  9.99 us
    all_to_all x1, starting transfers between devices, per_device(): sources_all = lax.all_to_all(source_blocks, 'dst', 0, 0)  9.58 us
    ppermute x3, waiting for transfers between devices, scatter_src(): lax.ppermute(sent[2 * k:2 * k + 2], 'src', x_step(k)).astype(jnp.float32)  5.81 us
    ppermute x3, starting transfers between devices, gather_src(): lax.ppermute(near, 'src', x_step(k))  4.83 us
    ppermute x1, waiting for transfers between devices, scatter_src(): far = lax.ppermute(here[1].astype(jnp.bfloat16), 'src', HALVES)  4.61 us
  transfers between devices with their start and end apart: 12, of which 6 were waited for; matrix products, arithmetic and copies ran while one was open for 3% of the time, Pallas kernels for 11%

profile of v2, /device:TPU:2, one launch (start us, length us, event | category | flops | bytes accessed | tf_op | source)
XLA Modules:
  0.0 139.1 jit_solution(8824995832839762910)
XLA Ops:
  0.6 2.0 %pack_tables.1 = (bf16[16,208,128]{2,1,0:T(8,128)(2,1)}, bf16[208,128]{1,0:T(8,128)(2,1)}) custom-call(f32[64,400]{1,0:T(8,128)} %table_ref.2, f32[64,400]{1,0:T(8,128)} %table_ref.3), custom_call_target="tpu_custom_call" | custom-call | tf_op jit(solution)/shard_map/pack_tables/pallas_call | solution.py:131
  2.6 9.6 %all-to-all-start = ((bf16[16,208,128]{2,1,0:T(8,128)(2,1)}), bf16[16,208,128]{2,1,0:T(8,128)(2,1)S(1)}, u32[]{:S(2)}, u32[]{:S(2)}) async-start(bf16[16,208,128]{2,1,0:T(8,128)(2,1)} %get-tuple-element.17), calls=%async_computation | async-start | bytes 1703936 | tf_op jit(solution)/shard_map/all_to_all | solution.py:324
  12.2 3.0 %collective-permute-start = (bf16[208,128]{1,0:T(8,128)(2,1)}, bf16[208,128]{1,0:T(8,128)(2,1)S(1)}, u32[]{:S(2)}, u32[]{:S(2)}) collective-permute-start(bf16[208,128]{1,0:T(8,128)(2,1)} %get-tuple-element.18), channel_id=1, source_target_pairs={{0,128},{16,144},{32,160},{48,176},{64,192},{80,208},{96,224},{112... | collective-permute-start | bytes 159752 | tf_op jit(solution)/shard_map/ppermute | solution.py:295
  15.2 0.8 constant_dynamic-update-slice_fusion.4
  16.7 2.4 %collective-permute-done = bf16[208,128]{1,0:T(8,128)(2,1)S(1)} collective-permute-done((bf16[208,128]{1,0:T(8,128)(2,1)}, bf16[208,128]{1,0:T(8,128)(2,1)S(1)}, u32[]{:S(2)}, u32[]{:S(2)}) %collective-permute-start) | collective-permute-done | bytes 53280 | tf_op jit(solution)/shard_map/ppermute | solution.py:295
  19.1 0.8 pad_maximum_fusion.1
  20.0 0.6 collective-permute-start.3
  20.6 2.4 %collective-permute-start.2 = (bf16[2,208,128]{2,1,0:T(8,128)(2,1)S(1)}, bf16[2,208,128]{2,1,0:T(8,128)(2,1)S(1)}, u32[]{:S(2)}, u32[]{:S(2)}) collective-permute-start(bf16[2,208,128]{2,1,0:T(8,128)(2,1)S(1)} %pad_maximum_fusion.1), channel_id=1, source_target_pairs={{0,64},{16,80},{32,96},{48,112},{64,0},{80,16},{96,32},{112,48},{1... | collective-permute-start | bytes 319496 | tf_op jit(solution)/shard_map/ppermute | solution.py:296
  23.0 1.8 %collective-permute-start.1 = (bf16[2,208,128]{2,1,0:T(8,128)(2,1)S(1)}, bf16[2,208,128]{2,1,0:T(8,128)(2,1)S(1)}, u32[]{:S(2)}, u32[]{:S(2)}) collective-permute-start(bf16[2,208,128]{2,1,0:T(8,128)(2,1)S(1)} %pad_maximum_fusion.1), channel_id=1, source_target_pairs={{0,32},{16,48},{32,64},{48,80},{64,96},{80,112},{96,0},{112,16},{1... | collective-permute-start | bytes 319496 | tf_op jit(solution)/shard_map/ppermute | solution.py:296
  24.8 3.1 %collective-permute-done.1 = bf16[2,208,128]{2,1,0:T(8,128)(2,1)S(1)} collective-permute-done((bf16[2,208,128]{2,1,0:T(8,128)(2,1)S(1)}, bf16[2,208,128]{2,1,0:T(8,128)(2,1)S(1)}, u32[]{:S(2)}, u32[]{:S(2)}) %collective-permute-start.1) | collective-permute-done | bytes 106528 | tf_op jit(solution)/shard_map/ppermute | solution.py:296
  28.0 0.0 collective-permute-done.2
  28.0 0.0 collective-permute-done.3
  28.0 0.0 copy-start.2
  28.0 0.1 collective-permute-start.4
  28.1 13.1 %pair_counts.1 = (bf16[4,1024,1024]{2,1,0:T(8,128)(2,1)}, bf16[4,1024,1024]{2,1,0:T(8,128)(2,1)}) custom-call(s32[12]{0:T(128)} %bitcast.27, s32[1]{0:T(128)} %bitcast.19.cnt_ref, s32[1,6144]{1,0:T(1,128)} %bitcast.24, s32[1,6144]{1,0:T(1,128)} %bitcast.25, s32[1,6144]{1,0:T(1,128)} %bitcast.26), custom_call_target="tpu_custom_call" | custom-call | flops 12884901888 | bytes 16777216 | tf_op jit(solution)/shard_map/pair_counts/pallas_call | solution.py:91
  41.3 0.0 copy-done.2
  41.3 0.0 collective-permute-done.4.t_other_ref
  41.3 0.0 copy-start.3
  41.3 0.0 all-to-all-done.s_ref
  41.3 0.0 copy-start.1
  41.3 0.7 copy-done.3
  42.1 0.3 copy-done.1
  42.4 27.2 %source_gradients.1 = (bf16[16,208,128]{2,1,0:T(8,128)(2,1)}, bf16[4,1024,1024]{2,1,0:T(8,128)(2,1)}, bf16[4,1024,400]{2,1,0:T(8,128)(2,1)}) custom-call(s32[1]{0:T(128)} %bitcast.member_ref, bf16[16,208,128]{2,1,0:T(8,128)(2,1)} %copy-done.1, bf16[8,208,128]{2,1,0:T(8,128)(2,1)} %copy-done.2, bf16[8,208,128]{2,1,0:T(8,128)(2,1)} %copy-done.3, ...), custom_call_target="tpu_custom_call" | custom-call | flops 12884901888 | bytes 33554432 | tf_op jit(solution)/shard_map/source_gradients/pallas_call | solution.py:189
  69.6 10.0 %target_gradients.1 = (bf16[8,208,128]{2,1,0:T(8,128)(2,1)}, bf16[8,208,128]{2,1,0:T(8,128)(2,1)}) custom-call(s32[1]{0:T(128)} %bitcast.member_ref, bf16[4,1024,1024]{2,1,0:T(8,128)(2,1)} %get-tuple-element.24.a_ref, bf16[4,1024,400]{2,1,0:T(8,128)(2,1)} %get-tuple-element.25.q_ref), custom_call_target="tpu_custom_call" | custom-call | flops 4294967296 | bytes 12582912 | tf_op jit(solution)/shard_map/target_gradients/pallas_call | solution.py:245
  79.6 2.9 %collective-permute-start.5 = (bf16[8,208,128]{2,1,0:T(8,128)(2,1)}, bf16[8,208,128]{2,1,0:T(8,128)(2,1)S(1)}, u32[]{:S(2)}, u32[]{:S(2)}) collective-permute-start(bf16[8,208,128]{2,1,0:T(8,128)(2,1)} %get-tuple-element.27), channel_id=1, source_target_pairs={{0,16},{16,0},{32,48},{48,32},{64,80},{80,64},{96,112},{112,96},{1... | collective-permute-start | bytes 1277960 | tf_op jit(solution)/shard_map/ppermute | solution.py:301
  82.5 29.6 %all-to-all-start.1 = ((bf16[16,208,128]{2,1,0:T(8,128)(2,1)}), bf16[16,208,128]{2,1,0:T(8,128)(2,1)S(1)}, u32[]{:S(2)}, u32[]{:S(2)}) async-start(bf16[16,208,128]{2,1,0:T(8,128)(2,1)} %get-tuple-element.21), calls=%async_computation.1 | async-start | bytes 1703936 | tf_op jit(solution)/shard_map/all_to_all | solution.py:335
  112.1 0.0 collective-permute-done.5
  112.1 1.1 fusion.3
  113.3 0.1 collective-permute-start.6
  113.4 2.0 %collective-permute-start.8 = (bf16[2,208,128]{2,1,0:T(8,128)(2,1)S(1)}, bf16[2,208,128]{2,1,0:T(8,128)(2,1)S(1)}, u32[]{:S(2)}, u32[]{:S(2)}) collective-permute-start(bf16[2,208,128]{2,1,0:T(8,128)(2,1)S(1)} %get-tuple-element.33), channel_id=1, source_target_pairs={{0,96},{16,112},{32,0},{48,16},{64,32},{80,48},{96,64},{112,80},{1... | collective-permute-start | bytes 319496 | tf_op jit(solution)/shard_map/ppermute | solution.py:305
  115.4 0.4 collective-permute-start.7
  115.8 3.1 %collective-permute-done.6 = bf16[2,208,128]{2,1,0:T(8,128)(2,1)S(1)} collective-permute-done((bf16[2,208,128]{2,1,0:T(8,128)(2,1)S(1)}, bf16[2,208,128]{2,1,0:T(8,128)(2,1)S(1)}, u32[]{:S(2)}, u32[]{:S(2)}) %collective-permute-start.6) | collective-permute-done | bytes 106528 | tf_op jit(solution)/shard_map/ppermute | solution.py:305
  118.8 0.0 collective-permute-done.8
  118.8 2.7 %collective-permute-done.7 = bf16[2,208,128]{2,1,0:T(8,128)(2,1)S(1)} collective-permute-done((bf16[2,208,128]{2,1,0:T(8,128)(2,1)S(1)}, bf16[2,208,128]{2,1,0:T(8,128)(2,1)S(1)}, u32[]{:S(2)}, u32[]{:S(2)}) %collective-permute-start.7) | collective-permute-done | bytes 106528 | tf_op jit(solution)/shard_map/ppermute | solution.py:305
  121.6 0.1 fusion.1
  121.7 2.3 %collective-permute-start.9 = (bf16[208,128]{1,0:T(8,128)(2,1)S(1)}, bf16[208,128]{1,0:T(8,128)(2,1)S(1)}, u32[]{:S(2)}, u32[]{:S(2)}) collective-permute-start(bf16[208,128]{1,0:T(8,128)(2,1)S(1)} %fusion.2), channel_id=1, source_target_pairs={{0,128},{16,144},{32,160},{48,176},{64,192},{80,208},{96,224},{112... | collective-permute-start | bytes 159752 | tf_op jit(solution)/shard_map/ppermute | solution.py:306
  124.0 4.6 %collective-permute-done.9 = bf16[208,128]{1,0:T(8,128)(2,1)S(1)} collective-permute-done((bf16[208,128]{1,0:T(8,128)(2,1)S(1)}, bf16[208,128]{1,0:T(8,128)(2,1)S(1)}, u32[]{:S(2)}, u32[]{:S(2)}) %collective-permute-start.9) | collective-permute-done | bytes 53280 | tf_op jit(solution)/shard_map/ppermute | solution.py:306
  128.6 0.7 pad_maximum_fusion.part_ref
  129.3 2.0 %row_adagrad.3 = (f32[64,400]{1,0:T(8,128)}, f32[1,64]{1,0:T(1,128)}) custom-call(f32[2,208,128]{2,1,0:T(8,128)} %pad_maximum_fusion.part_ref, f32[64,400]{1,0:T(8,128)} %table_ref.3, f32[1,64]{1,0:T(1,128)} %bitcast.23), custom_call_target="tpu_custom_call" | custom-call | flops 1048576 | bytes 2097152 | tf_op jit(solution)/shard_map/row_adagrad/pallas_call | solution.py:277
  131.3 4.5 %all-to-all-done.1.part_ref = bf16[16,208,128]{2,1,0:T(8,128)(2,1)S(1)} async-done(((bf16[16,208,128]{2,1,0:T(8,128)(2,1)}), bf16[16,208,128]{2,1,0:T(8,128)(2,1)S(1)}, u32[]{:S(2)}, u32[]{:S(2)}) %all-to-all-start.1) | async-done | bytes 852000 | tf_op jit(solution)/shard_map/all_to_all | solution.py:335
  135.8 0.0 copy-start
  135.8 0.9 copy-done
  136.7 2.3 %row_adagrad.2 = (f32[64,400]{1,0:T(8,128)}, f32[1,64]{1,0:T(1,128)}) custom-call(bf16[16,208,128]{2,1,0:T(8,128)(2,1)} %copy-done, f32[64,400]{1,0:T(8,128)} %table_ref.2, f32[1,64]{1,0:T(1,128)} %bitcast.22), custom_call_target="tpu_custom_call" | custom-call | flops 1048576 | bytes 2097152 | tf_op jit(solution)/shard_map/row_adagrad/pallas_call | solution.py:277
  (8 shorter events, 0.1 us)
Async XLA Ops:
  2.6 38.7 %all-to-all-start = ((bf16[16,208,128]{2,1,0:T(8,128)(2,1)}), bf16[16,208,128]{2,1,0:T(8,128)(2,1)S(1)}, u32[]{:S(2)}, u32[]{:S(2)}) async-start(bf16[16,208,128]{2,1,0:T(8,128)(2,1)} %get-tuple-element.17), calls=%async_computation | async-start | bytes 1703936 | tf_op jit(solution)/shard_map/all_to_all | solution.py:324
  12.2 6.9 %collective-permute-start = (bf16[208,128]{1,0:T(8,128)(2,1)}, bf16[208,128]{1,0:T(8,128)(2,1)S(1)}, u32[]{:S(2)}, u32[]{:S(2)}) collective-permute-start(bf16[208,128]{1,0:T(8,128)(2,1)} %get-tuple-element.18), channel_id=1, source_target_pairs={{0,128},{16,144},{32,160},{48,176},{64,192},{80,208},{96,224},{112... | collective-permute-start | bytes 159752 | tf_op jit(solution)/shard_map/ppermute | solution.py:295
  20.0 8.0 %collective-permute-start.3 = (bf16[2,208,128]{2,1,0:T(8,128)(2,1)S(1)}, bf16[2,208,128]{2,1,0:T(8,128)(2,1)S(1)}, u32[]{:S(2)}, u32[]{:S(2)}) collective-permute-start(bf16[2,208,128]{2,1,0:T(8,128)(2,1)S(1)} %pad_maximum_fusion.1), channel_id=1, source_target_pairs={{0,96},{16,112},{32,0},{48,16},{64,32},{80,48},{96,64},{112,80},{1... | collective-permute-start | bytes 319496 | tf_op jit(solution)/shard_map/ppermute | solution.py:296
  20.6 7.4 %collective-permute-start.2 = (bf16[2,208,128]{2,1,0:T(8,128)(2,1)S(1)}, bf16[2,208,128]{2,1,0:T(8,128)(2,1)S(1)}, u32[]{:S(2)}, u32[]{:S(2)}) collective-permute-start(bf16[2,208,128]{2,1,0:T(8,128)(2,1)S(1)} %pad_maximum_fusion.1), channel_id=1, source_target_pairs={{0,64},{16,80},{32,96},{48,112},{64,0},{80,16},{96,32},{112,48},{1... | collective-permute-start | bytes 319496 | tf_op jit(solution)/shard_map/ppermute | solution.py:296
  23.0 5.0 %collective-permute-start.1 = (bf16[2,208,128]{2,1,0:T(8,128)(2,1)S(1)}, bf16[2,208,128]{2,1,0:T(8,128)(2,1)S(1)}, u32[]{:S(2)}, u32[]{:S(2)}) collective-permute-start(bf16[2,208,128]{2,1,0:T(8,128)(2,1)S(1)} %pad_maximum_fusion.1), channel_id=1, source_target_pairs={{0,32},{16,48},{32,64},{48,80},{64,96},{80,112},{96,0},{112,16},{1... | collective-permute-start | bytes 319496 | tf_op jit(solution)/shard_map/ppermute | solution.py:296
  28.0 13.3 %copy-start.2 = (bf16[8,208,128]{2,1,0:T(8,128)(2,1)}, bf16[8,208,128]{2,1,0:T(8,128)(2,1)S(1)}, u32[]{:S(2)}) copy-start(bf16[8,208,128]{2,1,0:T(8,128)(2,1)S(1)} %constant_dynamic-update-slice_fusion.t_own_ref) | copy-start | bytes 1277956
  28.0 13.3 %collective-permute-start.4 = (bf16[8,208,128]{2,1,0:T(8,128)(2,1)S(1)}, bf16[8,208,128]{2,1,0:T(8,128)(2,1)S(1)}, u32[]{:S(2)}, u32[]{:S(2)}) collective-permute-start(bf16[8,208,128]{2,1,0:T(8,128)(2,1)S(1)} %constant_dynamic-update-slice_fusion.t_own_ref), channel_id=1, source_target_pairs={{0,16},{16,0},{32,48},{48,32},{64,80},{80,64},{96,112},{112,96},{1... | collective-permute-start | bytes 1277960 | tf_op jit(solution)/shard_map/ppermute | solution.py:297
  41.3 0.8 copy-start.3
  41.3 1.0 copy-start.1
  79.6 32.5 %collective-permute-start.5 = (bf16[8,208,128]{2,1,0:T(8,128)(2,1)}, bf16[8,208,128]{2,1,0:T(8,128)(2,1)S(1)}, u32[]{:S(2)}, u32[]{:S(2)}) collective-permute-start(bf16[8,208,128]{2,1,0:T(8,128)(2,1)} %get-tuple-element.27), channel_id=1, source_target_pairs={{0,16},{16,0},{32,48},{48,32},{64,80},{80,64},{96,112},{112,96},{1... | collective-permute-start | bytes 1277960 | tf_op jit(solution)/shard_map/ppermute | solution.py:301
  82.5 53.4 %all-to-all-start.1 = ((bf16[16,208,128]{2,1,0:T(8,128)(2,1)}), bf16[16,208,128]{2,1,0:T(8,128)(2,1)S(1)}, u32[]{:S(2)}, u32[]{:S(2)}) async-start(bf16[16,208,128]{2,1,0:T(8,128)(2,1)} %get-tuple-element.21), calls=%async_computation.1 | async-start | bytes 1703936 | tf_op jit(solution)/shard_map/all_to_all | solution.py:335
  113.3 5.6 %collective-permute-start.6 = (bf16[2,208,128]{2,1,0:T(8,128)(2,1)S(1)}, bf16[2,208,128]{2,1,0:T(8,128)(2,1)S(1)}, u32[]{:S(2)}, u32[]{:S(2)}) collective-permute-start(bf16[2,208,128]{2,1,0:T(8,128)(2,1)S(1)} %get-tuple-element.32), channel_id=1, source_target_pairs={{0,32},{16,48},{32,64},{48,80},{64,96},{80,112},{96,0},{112,16},{1... | collective-permute-start | bytes 319496 | tf_op jit(solution)/shard_map/ppermute | solution.py:305
  113.4 5.5 %collective-permute-start.8 = (bf16[2,208,128]{2,1,0:T(8,128)(2,1)S(1)}, bf16[2,208,128]{2,1,0:T(8,128)(2,1)S(1)}, u32[]{:S(2)}, u32[]{:S(2)}) collective-permute-start(bf16[2,208,128]{2,1,0:T(8,128)(2,1)S(1)} %get-tuple-element.33), channel_id=1, source_target_pairs={{0,96},{16,112},{32,0},{48,16},{64,32},{80,48},{96,64},{112,80},{1... | collective-permute-start | bytes 319496 | tf_op jit(solution)/shard_map/ppermute | solution.py:305
  115.4 6.2 %collective-permute-start.7 = (bf16[2,208,128]{2,1,0:T(8,128)(2,1)S(1)}, bf16[2,208,128]{2,1,0:T(8,128)(2,1)S(1)}, u32[]{:S(2)}, u32[]{:S(2)}) collective-permute-start(bf16[2,208,128]{2,1,0:T(8,128)(2,1)S(1)} %get-tuple-element.34), channel_id=1, source_target_pairs={{0,64},{16,80},{32,96},{48,112},{64,0},{80,16},{96,32},{112,48},{1... | collective-permute-start | bytes 319496 | tf_op jit(solution)/shard_map/ppermute | solution.py:305
  121.7 6.9 %collective-permute-start.9 = (bf16[208,128]{1,0:T(8,128)(2,1)S(1)}, bf16[208,128]{1,0:T(8,128)(2,1)S(1)}, u32[]{:S(2)}, u32[]{:S(2)}) collective-permute-start(bf16[208,128]{1,0:T(8,128)(2,1)S(1)} %fusion.2), channel_id=1, source_target_pairs={{0,128},{16,144},{32,160},{48,176},{64,192},{80,208},{96,224},{112... | collective-permute-start | bytes 159752 | tf_op jit(solution)/shard_map/ppermute | solution.py:306
  135.8 0.9 copy-start

commit v3 on v2

v3 whole, which is shorter than its diff:
```python
import jax
import jax.numpy as jnp
from jax import lax
from jax.experimental import pallas as pl
from jax.experimental.pallas import tpu as pltpu
from jax.sharding import PartitionSpec as P

BATCH = 512
NEG = 512
BATCHES = 12
NREL = 4
PART = 1024
DIM = 400
GROUP = 16
LINES = 208
TILE = 1024
COUNT_TILE = 256
ONE_HOT = jnp.float8_e4m3fn

learn_rate = 0.5
epsilon = 1e-08

NT = (((1,), (1,)), ((), ()))
TN = (((0,), (0,)), ((), ()))
COUNT_VMEM = 32 * 1024 * 1024
GRADIENT_VMEM = 48 * 1024 * 1024


def dot(a, b, dims=(((1,), (0,)), ((), ()))):
    return lax.dot_general(a, b, dims, preferred_element_type=jnp.float32)


def one_hot_columns(ids, rows, first, value, dtype):
    row = lax.broadcasted_iota(jnp.int32, (rows, ids.shape[1]), 0) + first
    return jnp.where(row == ids, jnp.float32(value), jnp.float32(0.0)).astype(dtype)


def histogram(ids, value):
    high = one_hot_columns(jnp.right_shift(ids, 7), 8, 0, 1.0, jnp.bfloat16)
    low = one_hot_columns(jnp.bitwise_and(ids, 127), 128, 0, value, jnp.bfloat16)
    table = dot(high, low, NT)
    return jnp.concatenate([table[k : k + 1] for k in range(8)], axis=1)


def count_kernel(rel_ref, cnt_ref, es_ref, et_ref, neg_ref, n_ref, m_ref, ohs, acc, srch, negh):
    step = pl.program_id(0)
    valid = cnt_ref[0]

    def sources_of(b):
        slot = lax.broadcasted_iota(jnp.int32, (1, BATCH), 1) + b * BATCH
        return jnp.where(slot < valid, es_ref[:, b * BATCH : (b + 1) * BATCH], -1)

    @pl.when(step == 0)
    def _():
        for b in range(BATCHES):
            ids = sources_of(b)
            column = jnp.broadcast_to(ids, (128, BATCH)).T[:, :1]
            lane = lax.broadcasted_iota(jnp.int32, (BATCH, PART), 1)
            ohs[b] = jnp.where(lane == column, jnp.float32(1.0), jnp.float32(0.0)).astype(ONE_HOT)
            srch[b : b + 1] = histogram(ids, 1.0)
            negh[b : b + 1] = histogram(neg_ref[:, b * BATCH : (b + 1) * BATCH], 1.0 / 1024.0)
        srch[BATCHES:] = jnp.zeros((16 - BATCHES, PART), jnp.float32)
        negh[BATCHES:] = jnp.zeros((16 - BATCHES, PART), jnp.float32)

    acc[...] = jnp.zeros_like(acc)
    for b in range(BATCHES):
        oht = one_hot_columns(et_ref[:, b * BATCH : (b + 1) * BATCH], COUNT_TILE, step * COUNT_TILE, 0.5, ONE_HOT)
        acc[rel_ref[b]] += dot(oht, ohs[b])

    n_ref[...] = acc[...].astype(jnp.bfloat16)
    lanes = pl.ds(pl.multiple_of(step * COUNT_TILE, COUNT_TILE), COUNT_TILE)
    negs = negh[:, lanes].astype(jnp.bfloat16)
    row = lax.broadcasted_iota(jnp.int32, (16, 1), 0)
    rel = jnp.full((16, 1), -1, jnp.int32)
    for b in range(BATCHES):
        rel = jnp.where(row == b, rel_ref[b], rel)
    for r in range(NREL):
        kept = jnp.where(rel == r, srch[...], 0.0).astype(jnp.bfloat16)
        m_ref[r] = dot(negs, kept, TN).astype(jnp.bfloat16)


def counts(rel, cnt, es, et, neg):
    smem = pl.BlockSpec(memory_space=pltpu.SMEM)
    whole = pl.BlockSpec((1, BATCHES * BATCH), lambda t: (0, 0))
    tiles = pl.BlockSpec((NREL, COUNT_TILE, PART), lambda t: (0, t, 0))
    out = jax.ShapeDtypeStruct((NREL, PART, PART), jnp.bfloat16)
    return pl.pallas_call(
        count_kernel,
        grid=(PART // COUNT_TILE,),
        in_specs=[smem, smem, whole, whole, whole],
        out_specs=[tiles, tiles],
        out_shape=[out, out],
        scratch_shapes=[
            pltpu.VMEM((BATCHES, BATCH, PART), ONE_HOT),
            pltpu.VMEM((NREL, COUNT_TILE, PART), jnp.float32),
            pltpu.VMEM((16, PART), jnp.float32),
            pltpu.VMEM((16, PART), jnp.float32),
        ],
        compiler_params=pltpu.CompilerParams(vmem_limit_bytes=COUNT_VMEM),
        cost_estimate=pl.CostEstimate(flops=2 * PART * PART * BATCHES * BATCH, bytes_accessed=16 << 20, transcendentals=0),
        name="pair_counts",
    )(rel, cnt, es, et, neg)


def pack(block):
    parts = [block[:, 128 * c : 128 * c + 128] for c in range(3)]
    tail = [block[16 * g : 16 * g + 16, 384:DIM] for g in range(4)]
    parts.append(jnp.concatenate(tail + [jnp.zeros((16, 64), block.dtype)], axis=1))
    return jnp.concatenate(parts, axis=0)


def unpack(lines):
    parts = [lines[64 * c : 64 * c + 64] for c in range(3)]
    tail = [lines[192:208, 16 * g : 16 * g + 16] for g in range(4)]
    parts.append(jnp.concatenate(tail, axis=0))
    return jnp.concatenate(parts, axis=1)


def pack_kernel(source_ref, target_ref, spread_ref, packed_ref):
    lines = pack(source_ref[...]).astype(jnp.bfloat16)
    for d in range(GROUP):
        spread_ref[d] = lines
    packed_ref[...] = pack(target_ref[...]).astype(jnp.bfloat16)


def pack_tables(source_table, target_table):
    return pl.pallas_call(
        pack_kernel,
        out_shape=[
            jax.ShapeDtypeStruct((GROUP, LINES, 128), jnp.bfloat16),
            jax.ShapeDtypeStruct((LINES, 128), jnp.bfloat16),
        ],
        name="pack_tables",
    )(source_table, target_table)


def place(member, near, other):
    high, x, core = member // 8, (member // 2) % 4, member % 2
    return jnp.bitwise_xor(high, near % 2) * 8 + ((x + 4 - near // 2) % 4) * 2 + jnp.bitwise_xor(core, other)


def gradient_kernel(
    member_ref, s_ref, t_own_ref, t_other_ref, rel_ref, n_ref, m_ref, gs_ref, own_ref, other_ref,
    s, half, tt, q0, q1, a0, a1, sacc, tacc,
):
    r, k = pl.program_id(0), pl.program_id(1)
    member = member_ref[0]
    high, x, core = member // 8, (member // 2) % 4, member % 2
    tile = pl.ds(pl.multiple_of(k * TILE, TILE), TILE)
    qs, coefs = (q0, q1), (a0, a1)

    @pl.when((r == 0) & (k == 0))
    def _():
        for d in range(GROUP):
            s[64 * d : 64 * d + 64] = unpack(s_ref[d])
        for other, ref in enumerate((t_own_ref, t_other_ref)):
            for near in range(8):
                first = pl.multiple_of(place(member, near, other) * 64, 64)
                half[pl.ds(first, 64)] = unpack(ref[near])
        tt[...] = half[...].astype(jnp.float32).T.astype(jnp.bfloat16)
        half[...] = half[...] * jnp.bfloat16(0.5)
        sacc[...] = jnp.zeros_like(sacc)
        tacc[...] = jnp.zeros_like(tacc)
        q0[...] = dot(s[...], rel_ref[0]).astype(jnp.bfloat16)

    def targets_part(i):
        q = qs[i % 2]
        th = jnp.tanh(dot(half[tile], q[...], NT))
        coef = n_ref[0].astype(jnp.float32) * (th - 1.0) + m_ref[0].astype(jnp.float32) * (th + 1.0)
        coef = coef.astype(jnp.bfloat16)
        coefs[i % 2][tile] = coef
        if i + 1 < NREL:
            qs[(i + 1) % 2][tile] = dot(s[tile], rel_ref[i + 1]).astype(jnp.bfloat16)
        grad = tacc[tile] + dot(coef, q[...])
        if i + 1 < NREL:
            tacc[tile] = grad
            return
        grad = grad.astype(jnp.bfloat16)
        for u in range(TILE // 64):
            at = k * (TILE // 64) + u
            near = (((at // 2) % 4 + 4 - x) % 4) * 2 + jnp.bitwise_xor(at // 8, high)
            lines = pack(grad[64 * u : 64 * u + 64])

            @pl.when(core == u % 2)
            def _():
                own_ref[near] = lines

            @pl.when(core != u % 2)
            def _():
                other_ref[near] = lines

    def sources_part(i):
        query_grad = dot(tt[...], coefs[i % 2][:, tile]).astype(jnp.bfloat16)
        grad = sacc[:, tile] + dot(rel_ref[i], query_grad)
        if i + 1 < NREL:
            sacc[:, tile] = grad
            return
        grad = grad.T.astype(jnp.bfloat16)
        for u in range(TILE // 64):
            gs_ref[k * (TILE // 64) + u] = pack(grad[64 * u : 64 * u + 64])

    for i in range(NREL + 1):

        @pl.when(r == i)
        def _():
            if i > 0:
                sources_part(i - 1)
            if i < NREL:
                targets_part(i)


def gradients(member, sources, targets_own, targets_other, relations, n, m):
    tiles = pl.BlockSpec(
        (1, TILE, PART),
        lambda r, k: (jnp.minimum(r, NREL - 1), jnp.where(r == NREL, PART // TILE - 1, k), 0),
    )

    def blocks(count):
        return pl.BlockSpec((count, LINES, 128), lambda r, k: (0, 0, 0))

    wide = pltpu.VMEM((PART, DIM), jnp.bfloat16)
    square = pltpu.VMEM((PART, PART), jnp.bfloat16)
    return pl.pallas_call(
        gradient_kernel,
        grid=(NREL + 1, PART // TILE),
        in_specs=[
            pl.BlockSpec(memory_space=pltpu.SMEM),
            blocks(GROUP),
            blocks(8),
            blocks(8),
            pl.BlockSpec((NREL, DIM, DIM), lambda r, k: (0, 0, 0)),
            tiles,
            tiles,
        ],
        out_specs=[blocks(GROUP), blocks(8), blocks(8)],
        out_shape=[
            jax.ShapeDtypeStruct((GROUP, LINES, 128), jnp.bfloat16),
            jax.ShapeDtypeStruct((8, LINES, 128), jnp.bfloat16),
            jax.ShapeDtypeStruct((8, LINES, 128), jnp.bfloat16),
        ],
        scratch_shapes=[
            wide,
            wide,
            pltpu.VMEM((DIM, PART), jnp.bfloat16),
            wide,
            wide,
            square,
            square,
            pltpu.VMEM((DIM, PART), jnp.float32),
            pltpu.VMEM((PART, DIM), jnp.float32),
        ],
        compiler_params=pltpu.CompilerParams(vmem_limit_bytes=GRADIENT_VMEM),
        cost_estimate=pl.CostEstimate(flops=16 << 30, bytes_accessed=20 << 20, transcendentals=4 << 20),
        name="gradients",
    )(member, sources, targets_own, targets_other, relations, n, m)


def update_kernel(part_ref, table_ref, state_ref, new_table_ref, new_state_ref):
    lines = part_ref[0].astype(jnp.float32)
    for k in range(1, part_ref.shape[0]):
        lines = lines + part_ref[k].astype(jnp.float32)
    grad = unpack(lines)
    rows = grad.shape[0]
    mean = jnp.sum(grad * grad, axis=1, keepdims=True) / DIM
    mean_row = jnp.broadcast_to(mean, (rows, 128)).T[:1]
    new_state_row = state_ref[...] + mean_row
    new_state_ref[...] = new_state_row
    new_state = jnp.broadcast_to(new_state_row, (128, rows)).T[:, :1]
    new_table_ref[...] = table_ref[...] - learn_rate * grad / (jnp.sqrt(new_state) + epsilon)


def update(parts, table, state):
    rows = table.shape[0]
    new_table, new_state = pl.pallas_call(
        update_kernel,
        out_shape=[jax.ShapeDtypeStruct(table.shape, jnp.float32), jax.ShapeDtypeStruct((1, rows), jnp.float32)],
        cost_estimate=pl.CostEstimate(flops=1 << 20, bytes_accessed=2 << 20, transcendentals=0),
        name="row_adagrad",
    )(parts, table, state.reshape(1, rows))
    return new_table, new_state.reshape(rows)


HALVES = [(i, i ^ 8) for i in range(16)]
CORES = [(i, i ^ 1) for i in range(16)]


def x_step(k):
    return [(i, (i & 9) | ((((i >> 1) + k) & 3) << 1)) for i in range(16)]


def gather_src(lines):
    near = jnp.stack([lines, lax.ppermute(lines, "src", HALVES)])
    own = jnp.concatenate([near] + [lax.ppermute(near, "src", x_step(k)) for k in (1, 2, 3)])
    return own, lax.ppermute(own, "src", CORES)


def scatter_src(own, other):
    total = own.astype(jnp.float32) + lax.ppermute(other, "src", CORES).astype(jnp.float32)
    sent = total.astype(jnp.bfloat16)
    here = total[:2]
    for k in (1, 2, 3):
        here = here + lax.ppermute(sent[2 * k : 2 * k + 2], "src", x_step(k)).astype(jnp.float32)
    far = lax.ppermute(here[1].astype(jnp.bfloat16), "src", HALVES)
    return jnp.stack([here[0], far.astype(jnp.float32)])


def per_device(
    source_table,
    source_state,
    target_table,
    target_state,
    relations,
    edge_source,
    edge_target,
    batch_relation,
    edge_counts,
    negatives,
):
    member = lax.axis_index("src").reshape(1)
    source_blocks, target_lines = pack_tables(source_table, target_table)
    sources_all = lax.all_to_all(source_blocks, "dst", 0, 0)
    targets_own, targets_other = gather_src(target_lines)
    slots = (1, BATCHES * BATCH)
    n, m = counts(
        batch_relation.reshape(BATCHES),
        edge_counts.reshape(1),
        edge_source.reshape(slots),
        edge_target.reshape(slots),
        negatives.reshape(slots),
    )
    source_grad, own, other = gradients(member, sources_all, targets_own, targets_other, relations, n, m)
    source_parts = lax.all_to_all(source_grad, "dst", 0, 0)
    target_parts = scatter_src(own, other)
    new_source_table, new_source_state = update(source_parts, source_table, source_state)
    new_target_table, new_target_state = update(target_parts, target_table, target_state)
    return (new_source_table, new_source_state, new_target_table, new_target_state)


def solution(mesh):
    return jax.shard_map(
        per_device,
        mesh=mesh,
        in_specs=(
            P(("src", "dst"), None),
            P(("src", "dst")),
            P(("dst", "src"), None),
            P(("dst", "src")),
            P(),
            P("src", "dst", None),
            P("src", "dst", None),
            P("src", "dst", None),
            P("src", "dst"),
            P("src", "dst", None, None),
        ),
        out_specs=(
            P(("src", "dst"), None),
            P(("src", "dst")),
            P(("dst", "src"), None),
            P(("dst", "src")),
        ),
        check_vma=False,
    )
```

time: 140 us -> 116 us (0.83)
  starting transfers between devices: 54.8 us -> 33.7 us
  Pallas kernels: 56.7 us -> 46.1 us
  local copies, waits for them, and re-layouts: 2.91 us -> 13 us
  waiting for transfers between devices: 20.5 us -> 18.4 us
    all_to_all x1, starting transfers between devices: 29.6 us -> 8.41 us  [per_device(): source_parts = lax.all_to_all(source_grad, 'dst', 0, 0)]
    pallas_call x3 -> x2, Pallas kernels: 50.3 us -> 39.7 us  [the longest x1 22.4 us: gradients(): pl.pallas_call(gradient_kernel, grid=(NREL + 1, PART // TILE), in_specs=[...]
    unnamed x12 -> x24, local copies, waits for them, and re-layouts: 2.85 us -> 13 us
    ppermute x1, starting transfers between devices: 2.9 us -> 0.43 us  [scatter_src(): lax.ppermute(other, 'src', CORES).astype(jnp.float32)]
    ppermute x3, starting transfers between devices: 2.49 us -> 4.87 us  [scatter_src(): lax.ppermute(sent[2 * k:2 * k + 2], 'src', x_step(k)).astype(jnp.float32)]
  transfers between devices with their start and end apart: 12 -> 12, of which waited for: 6 -> 7; matrix products, arithmetic and copies ran while one was open for 3% -> 2% of each run, Pallas kernels for 11% -> 17%
where the time goes in v3:
time: 116 us; the launch traced here: 114 us
  Pallas kernels  46.1 us (40%)
  starting transfers between devices  33.7 us (29%)
  waiting for transfers between devices  18.4 us (16%)
  local copies, waits for them, and re-layouts  13 us (11%)
  other arithmetic  1.7 us (1%)
  between operations  1.43 us (1%)
    pallas_call x1, Pallas kernels, gradients(): pl.pallas_call(gradient_kernel, grid=(NREL + 1, PART // TILE), in_specs=[...  22.4 us
    pallas_call x1, Pallas kernels, counts(): pl.pallas_call(count_kernel, grid=(PART // COUNT_TILE,), in_specs=[smem,...  17.4 us
    unnamed x24, local copies, waits for them, and re-layouts  13 us
    all_to_all x1, starting transfers between devices, per_device(): sources_all = lax.all_to_all(source_blocks, 'dst', 0, 0)  9.58 us
    all_to_all x1, starting transfers between devices, per_device(): source_parts = lax.all_to_all(source_grad, 'dst', 0, 0)  8.41 us
    ppermute x3, waiting for transfers between devices, scatter_src(): lax.ppermute(sent[2 * k:2 * k + 2], 'src', x_step(k)).astype(jnp.float32)  4.96 us
    ppermute x3, starting transfers between devices, scatter_src(): lax.ppermute(sent[2 * k:2 * k + 2], 'src', x_step(k)).astype(jnp.float32)  4.87 us
    ppermute x3, starting transfers between devices, gather_src(): lax.ppermute(near, 'src', x_step(k))  4.83 us
  transfers between devices with their start and end apart: 12, of which 7 were waited for; matrix products, arithmetic and copies ran while one was open for 2% of the time, Pallas kernels for 17%

profile of v3, /device:TPU:2, one launch (start us, length us, event | category | flops | bytes accessed | tf_op | source)
XLA Modules:
  0.0 114.3 jit_solution(8338429139492159325)
XLA Ops:
  0.6 2.0 %pack_tables.1 = (bf16[16,208,128]{2,1,0:T(8,128)(2,1)}, bf16[208,128]{1,0:T(8,128)(2,1)}) custom-call(f32[64,400]{1,0:T(8,128)} %table_ref.2, f32[64,400]{1,0:T(8,128)} %table_ref.3), custom_call_target="tpu_custom_call" | custom-call | tf_op jit(solution)/shard_map/pack_tables/pallas_call | solution.py:127
  2.6 9.6 %all-to-all-start = ((bf16[16,208,128]{2,1,0:T(8,128)(2,1)}), bf16[16,208,128]{2,1,0:T(8,128)(2,1)S(1)}, u32[]{:S(2)}, u32[]{:S(2)}) async-start(bf16[16,208,128]{2,1,0:T(8,128)(2,1)} %get-tuple-element.15), calls=%async_computation | async-start | bytes 1703936 | tf_op jit(solution)/shard_map/all_to_all | solution.py:321
  12.2 3.0 %collective-permute-start = (bf16[208,128]{1,0:T(8,128)(2,1)}, bf16[208,128]{1,0:T(8,128)(2,1)S(1)}, u32[]{:S(2)}, u32[]{:S(2)}) collective-permute-start(bf16[208,128]{1,0:T(8,128)(2,1)} %get-tuple-element.16), channel_id=1, source_target_pairs={{0,128},{16,144},{32,160},{48,176},{64,192},{80,208},{96,224},{112... | collective-permute-start | bytes 159752 | tf_op jit(solution)/shard_map/ppermute | solution.py:292
  15.2 0.8 constant_dynamic-update-slice_fusion.4
  16.7 2.4 %collective-permute-done = bf16[208,128]{1,0:T(8,128)(2,1)S(1)} collective-permute-done((bf16[208,128]{1,0:T(8,128)(2,1)}, bf16[208,128]{1,0:T(8,128)(2,1)S(1)}, u32[]{:S(2)}, u32[]{:S(2)}) %collective-permute-start) | collective-permute-done | bytes 53280 | tf_op jit(solution)/shard_map/ppermute | solution.py:292
  19.1 0.8 pad_maximum_fusion.1
  20.0 0.6 collective-permute-start.3
  20.6 2.4 %collective-permute-start.2 = (bf16[2,208,128]{2,1,0:T(8,128)(2,1)S(1)}, bf16[2,208,128]{2,1,0:T(8,128)(2,1)S(1)}, u32[]{:S(2)}, u32[]{:S(2)}) collective-permute-start(bf16[2,208,128]{2,1,0:T(8,128)(2,1)S(1)} %pad_maximum_fusion.1), channel_id=1, source_target_pairs={{0,64},{16,80},{32,96},{48,112},{64,0},{80,16},{96,32},{112,48},{1... | collective-permute-start | bytes 319496 | tf_op jit(solution)/shard_map/ppermute | solution.py:293
  23.0 1.8 %collective-permute-start.1 = (bf16[2,208,128]{2,1,0:T(8,128)(2,1)S(1)}, bf16[2,208,128]{2,1,0:T(8,128)(2,1)S(1)}, u32[]{:S(2)}, u32[]{:S(2)}) collective-permute-start(bf16[2,208,128]{2,1,0:T(8,128)(2,1)S(1)} %pad_maximum_fusion.1), channel_id=1, source_target_pairs={{0,32},{16,48},{32,64},{48,80},{64,96},{80,112},{96,0},{112,16},{1... | collective-permute-start | bytes 319496 | tf_op jit(solution)/shard_map/ppermute | solution.py:293
  24.8 3.1 %collective-permute-done.1 = bf16[2,208,128]{2,1,0:T(8,128)(2,1)S(1)} collective-permute-done((bf16[2,208,128]{2,1,0:T(8,128)(2,1)S(1)}, bf16[2,208,128]{2,1,0:T(8,128)(2,1)S(1)}, u32[]{:S(2)}, u32[]{:S(2)}) %collective-permute-start.1) | collective-permute-done | bytes 106528 | tf_op jit(solution)/shard_map/ppermute | solution.py:293
  28.0 0.0 collective-permute-done.2
  28.0 0.0 collective-permute-done.3
  28.0 0.1 collective-permute-start.4
  28.1 0.0 copy-start.3
  28.2 0.7 copy-done.3
  28.9 0.0 copy-start.4
  28.9 0.7 copy-done.4
  29.6 0.0 copy-start.5
  29.6 0.7 copy-done.5
  30.4 0.7 copy-done.6
  31.0 17.4 %pair_counts.1 = (bf16[4,1024,1024]{2,1,0:T(8,128)(2,1)S(1)}, bf16[4,1024,1024]{2,1,0:T(8,128)(2,1)S(1)}) custom-call(s32[12]{0:T(128)S(1)} %bitcast.23, s32[1]{0:T(128)} %bitcast.19.cnt_ref, s32[1,6144]{1,0:T(1,128)S(1)} %bitcast.20, s32[1,6144]{1,0:T(1,128)S(1)} %bitcast.21, s32[1,6144]{1,0:T(1,128)S(1)} %bitcast.22), custom_call_target="tpu_custom_call" | custom-call | flops 12884901888 | bytes 16777216 | tf_op jit(solution)/shard_map/pair_counts/pallas_call | solution.py:87
  48.4 0.0 copy-start.7
  48.4 3.3 %copy-done.7 = bf16[4,1024,1024]{2,1,0:T(8,128)(2,1)} copy-done((bf16[4,1024,1024]{2,1,0:T(8,128)(2,1)}, bf16[4,1024,1024]{2,1,0:T(8,128)(2,1)S(1)}, u32[]{:S(2)}) %copy-start.7) | copy-done | bytes 8388632
  51.7 3.2 %copy-done.8 = bf16[4,1024,1024]{2,1,0:T(8,128)(2,1)} copy-done((bf16[4,1024,1024]{2,1,0:T(8,128)(2,1)}, bf16[4,1024,1024]{2,1,0:T(8,128)(2,1)S(1)}, u32[]{:S(2)}) %copy-start.8) | copy-done | bytes 8388632
  54.9 0.0 collective-permute-done.4.t_other_ref
  54.9 0.8 copy-done.1
  55.7 0.0 all-to-all-done.s_ref
  55.7 0.0 copy-done
  55.7 1.0 copy-done.2
  56.7 22.4 %gradients.1 = (bf16[16,208,128]{2,1,0:T(8,128)(2,1)}, bf16[8,208,128]{2,1,0:T(8,128)(2,1)S(1)}, bf16[8,208,128]{2,1,0:T(8,128)(2,1)}) custom-call(s32[1]{0:T(128)} %bitcast.member_ref, bf16[16,208,128]{2,1,0:T(8,128)(2,1)S(1)} %all-to-all-done.s_ref, bf16[8,208,128]{2,1,0:T(8,128)(2,1)S(1)} %constant_dynamic-update-slice_fusion.t_own_ref, ...), custom_call_target="tpu_custom_call" | custom-call | flops 17179869184 | bytes 20971520 | tf_op jit(solution)/shard_map/gradients/pallas_call | solution.py:223
  79.1 0.4 collective-permute-start.5
  79.5 8.4 %all-to-all-start.1 = ((bf16[16,208,128]{2,1,0:T(8,128)(2,1)}), bf16[16,208,128]{2,1,0:T(8,128)(2,1)S(1)}, u32[]{:S(2)}, u32[]{:S(2)}) async-start(bf16[16,208,128]{2,1,0:T(8,128)(2,1)} %get-tuple-element.19), calls=%async_computation.1 | async-start | bytes 1703936 | tf_op jit(solution)/shard_map/all_to_all | solution.py:332
  87.9 0.0 collective-permute-done.5
  87.9 0.1 fusion.3
  88.1 1.6 %collective-permute-start.6 = (bf16[2,208,128]{2,1,0:T(8,128)(2,1)S(1)}, bf16[2,208,128]{2,1,0:T(8,128)(2,1)S(1)}, u32[]{:S(2)}, u32[]{:S(2)}) collective-permute-start(bf16[2,208,128]{2,1,0:T(8,128)(2,1)S(1)} %get-tuple-element.28), channel_id=1, source_target_pairs={{0,32},{16,48},{32,64},{48,80},{64,96},{80,112},{96,0},{112,16},{1... | collective-permute-start | bytes 319496 | tf_op jit(solution)/shard_map/ppermute | solution.py:302
  89.7 1.3 %collective-permute-start.8 = (bf16[2,208,128]{2,1,0:T(8,128)(2,1)S(1)}, bf16[2,208,128]{2,1,0:T(8,128)(2,1)S(1)}, u32[]{:S(2)}, u32[]{:S(2)}) collective-permute-start(bf16[2,208,128]{2,1,0:T(8,128)(2,1)S(1)} %get-tuple-element.29), channel_id=1, source_target_pairs={{0,96},{16,112},{32,0},{48,16},{64,32},{80,48},{96,64},{112,80},{1... | collective-permute-start | bytes 319496 | tf_op jit(solution)/shard_map/ppermute | solution.py:302
  91.0 2.0 %collective-permute-start.7 = (bf16[2,208,128]{2,1,0:T(8,128)(2,1)S(1)}, bf16[2,208,128]{2,1,0:T(8,128)(2,1)S(1)}, u32[]{:S(2)}, u32[]{:S(2)}) collective-permute-start(bf16[2,208,128]{2,1,0:T(8,128)(2,1)S(1)} %get-tuple-element.30), channel_id=1, source_target_pairs={{0,64},{16,80},{32,96},{48,112},{64,0},{80,16},{96,32},{112,48},{1... | collective-permute-start | bytes 319496 | tf_op jit(solution)/shard_map/ppermute | solution.py:302
  93.0 0.9 collective-permute-done.6
  93.8 0.6 collective-permute-done.8
  94.4 3.5 %collective-permute-done.7 = bf16[2,208,128]{2,1,0:T(8,128)(2,1)S(1)} collective-permute-done((bf16[2,208,128]{2,1,0:T(8,128)(2,1)S(1)}, bf16[2,208,128]{2,1,0:T(8,128)(2,1)S(1)}, u32[]{:S(2)}, u32[]{:S(2)}) %collective-permute-start.7) | collective-permute-done | bytes 106528 | tf_op jit(solution)/shard_map/ppermute | solution.py:302
  97.9 0.1 fusion.1
  98.0 2.5 %collective-permute-start.9 = (bf16[208,128]{1,0:T(8,128)(2,1)S(1)}, bf16[208,128]{1,0:T(8,128)(2,1)S(1)}, u32[]{:S(2)}, u32[]{:S(2)}) collective-permute-start(bf16[208,128]{1,0:T(8,128)(2,1)S(1)} %fusion.2), channel_id=1, source_target_pairs={{0,128},{16,144},{32,160},{48,176},{64,192},{80,208},{96,224},{112... | collective-permute-start | bytes 159752 | tf_op jit(solution)/shard_map/ppermute | solution.py:303
  100.5 3.9 %collective-permute-done.9 = bf16[208,128]{1,0:T(8,128)(2,1)S(1)} collective-permute-done((bf16[208,128]{1,0:T(8,128)(2,1)S(1)}, bf16[208,128]{1,0:T(8,128)(2,1)S(1)}, u32[]{:S(2)}, u32[]{:S(2)}) %collective-permute-start.9) | collective-permute-done | bytes 53280 | tf_op jit(solution)/shard_map/ppermute | solution.py:303
  104.5 0.7 pad_maximum_fusion.part_ref
  105.2 2.0 %row_adagrad.3 = (f32[64,400]{1,0:T(8,128)}, f32[1,64]{1,0:T(1,128)}) custom-call(f32[2,208,128]{2,1,0:T(8,128)} %pad_maximum_fusion.part_ref, f32[64,400]{1,0:T(8,128)} %table_ref.3, f32[1,64]{1,0:T(1,128)} %bitcast.27), custom_call_target="tpu_custom_call" | custom-call | flops 1048576 | bytes 2097152 | tf_op jit(solution)/shard_map/row_adagrad/pallas_call | solution.py:274
  107.2 3.9 %all-to-all-done.1.part_ref = bf16[16,208,128]{2,1,0:T(8,128)(2,1)S(1)} async-done(((bf16[16,208,128]{2,1,0:T(8,128)(2,1)}), bf16[16,208,128]{2,1,0:T(8,128)(2,1)S(1)}, u32[]{:S(2)}, u32[]{:S(2)}) %all-to-all-start.1) | async-done | bytes 852000 | tf_op jit(solution)/shard_map/all_to_all | solution.py:332
  111.1 0.9 copy-done.9
  112.0 2.3 %row_adagrad.2 = (f32[64,400]{1,0:T(8,128)}, f32[1,64]{1,0:T(1,128)}) custom-call(bf16[16,208,128]{2,1,0:T(8,128)(2,1)} %copy-done.9, f32[64,400]{1,0:T(8,128)} %table_ref.2, f32[1,64]{1,0:T(1,128)} %bitcast.26), custom_call_target="tpu_custom_call" | custom-call | flops 1048576 | bytes 2097152 | tf_op jit(solution)/shard_map/row_adagrad/pallas_call | solution.py:274
  (14 shorter events, 0.1 us)
Async XLA Ops:
  2.6 53.1 %all-to-all-start = ((bf16[16,208,128]{2,1,0:T(8,128)(2,1)}), bf16[16,208,128]{2,1,0:T(8,128)(2,1)S(1)}, u32[]{:S(2)}, u32[]{:S(2)}) async-start(bf16[16,208,128]{2,1,0:T(8,128)(2,1)} %get-tuple-element.15), calls=%async_computation | async-start | bytes 1703936 | tf_op jit(solution)/shard_map/all_to_all | solution.py:321
  12.2 6.9 %collective-permute-start = (bf16[208,128]{1,0:T(8,128)(2,1)}, bf16[208,128]{1,0:T(8,128)(2,1)S(1)}, u32[]{:S(2)}, u32[]{:S(2)}) collective-permute-start(bf16[208,128]{1,0:T(8,128)(2,1)} %get-tuple-element.16), channel_id=1, source_target_pairs={{0,128},{16,144},{32,160},{48,176},{64,192},{80,208},{96,224},{112... | collective-permute-start | bytes 159752 | tf_op jit(solution)/shard_map/ppermute | solution.py:292
  20.0 8.0 %collective-permute-start.3 = (bf16[2,208,128]{2,1,0:T(8,128)(2,1)S(1)}, bf16[2,208,128]{2,1,0:T(8,128)(2,1)S(1)}, u32[]{:S(2)}, u32[]{:S(2)}) collective-permute-start(bf16[2,208,128]{2,1,0:T(8,128)(2,1)S(1)} %pad_maximum_fusion.1), channel_id=1, source_target_pairs={{0,96},{16,112},{32,0},{48,16},{64,32},{80,48},{96,64},{112,80},{1... | collective-permute-start | bytes 319496 | tf_op jit(solution)/shard_map/ppermute | solution.py:293
  20.6 7.4 %collective-permute-start.2 = (bf16[2,208,128]{2,1,0:T(8,128)(2,1)S(1)}, bf16[2,208,128]{2,1,0:T(8,128)(2,1)S(1)}, u32[]{:S(2)}, u32[]{:S(2)}) collective-permute-start(bf16[2,208,128]{2,1,0:T(8,128)(2,1)S(1)} %pad_maximum_fusion.1), channel_id=1, source_target_pairs={{0,64},{16,80},{32,96},{48,112},{64,0},{80,16},{96,32},{112,48},{1... | collective-permute-start | bytes 319496 | tf_op jit(solution)/shard_map/ppermute | solution.py:293
  23.0 5.0 %collective-permute-start.1 = (bf16[2,208,128]{2,1,0:T(8,128)(2,1)S(1)}, bf16[2,208,128]{2,1,0:T(8,128)(2,1)S(1)}, u32[]{:S(2)}, u32[]{:S(2)}) collective-permute-start(bf16[2,208,128]{2,1,0:T(8,128)(2,1)S(1)} %pad_maximum_fusion.1), channel_id=1, source_target_pairs={{0,32},{16,48},{32,64},{48,80},{64,96},{80,112},{96,0},{112,16},{1... | collective-permute-start | bytes 319496 | tf_op jit(solution)/shard_map/ppermute | solution.py:293
  28.0 26.9 %collective-permute-start.4 = (bf16[8,208,128]{2,1,0:T(8,128)(2,1)S(1)}, bf16[8,208,128]{2,1,0:T(8,128)(2,1)S(1)}, u32[]{:S(2)}, u32[]{:S(2)}) collective-permute-start(bf16[8,208,128]{2,1,0:T(8,128)(2,1)S(1)} %constant_dynamic-update-slice_fusion.t_own_ref), channel_id=1, source_target_pairs={{0,16},{16,0},{32,48},{48,32},{64,80},{80,64},{96,112},{112,96},{1... | collective-permute-start | bytes 1277960 | tf_op jit(solution)/shard_map/ppermute | solution.py:294
  28.1 0.7 copy-start.3
  28.9 0.7 copy-start.4
  29.6 0.7 copy-start.5
  30.4 0.7 copy-start.6
  31.0 24.7 %copy-start = (bf16[4,400,400]{2,1,0:T(8,128)(2,1)S(1)}, bf16[4,400,400]{2,1,0:T(8,128)(2,1)}, u32[]{:S(2)}) copy-start(bf16[4,400,400]{2,1,0:T(8,128)(2,1)} %rel_ref.1) | copy-start | bytes 3840004
  48.4 3.3 %copy-start.7 = (bf16[4,1024,1024]{2,1,0:T(8,128)(2,1)}, bf16[4,1024,1024]{2,1,0:T(8,128)(2,1)S(1)}, u32[]{:S(2)}) copy-start(bf16[4,1024,1024]{2,1,0:T(8,128)(2,1)S(1)} %get-tuple-element.17.n_ref) | copy-start | bytes 25165828
  51.7 3.2 %copy-start.8 = (bf16[4,1024,1024]{2,1,0:T(8,128)(2,1)}, bf16[4,1024,1024]{2,1,0:T(8,128)(2,1)S(1)}, u32[]{:S(2)}) copy-start(bf16[4,1024,1024]{2,1,0:T(8,128)(2,1)S(1)} %get-tuple-element.18.m_ref) | copy-start | bytes 25165828
  54.9 0.8 copy-start.1
  55.7 1.0 copy-start.2
  79.1 8.8 %collective-permute-start.5 = (bf16[8,208,128]{2,1,0:T(8,128)(2,1)}, bf16[8,208,128]{2,1,0:T(8,128)(2,1)S(1)}, u32[]{:S(2)}, u32[]{:S(2)}) collective-permute-start(bf16[8,208,128]{2,1,0:T(8,128)(2,1)} %get-tuple-element.23), channel_id=1, source_target_pairs={{0,16},{16,0},{32,48},{48,32},{64,80},{80,64},{96,112},{112,96},{1... | collective-permute-start | bytes 1277960 | tf_op jit(solution)/shard_map/ppermute | solution.py:298
  79.5 31.6 %all-to-all-start.1 = ((bf16[16,208,128]{2,1,0:T(8,128)(2,1)}), bf16[16,208,128]{2,1,0:T(8,128)(2,1)S(1)}, u32[]{:S(2)}, u32[]{:S(2)}) async-start(bf16[16,208,128]{2,1,0:T(8,128)(2,1)} %get-tuple-element.19), calls=%async_computation.1 | async-start | bytes 1703936 | tf_op jit(solution)/shard_map/all_to_all | solution.py:332
  88.1 5.7 %collective-permute-start.6 = (bf16[2,208,128]{2,1,0:T(8,128)(2,1)S(1)}, bf16[2,208,128]{2,1,0:T(8,128)(2,1)S(1)}, u32[]{:S(2)}, u32[]{:S(2)}) collective-permute-start(bf16[2,208,128]{2,1,0:T(8,128)(2,1)S(1)} %get-tuple-element.28), channel_id=1, source_target_pairs={{0,32},{16,48},{32,64},{48,80},{64,96},{80,112},{96,0},{112,16},{1... | collective-permute-start | bytes 319496 | tf_op jit(solution)/shard_map/ppermute | solution.py:302
  89.7 4.7 %collective-permute-start.8 = (bf16[2,208,128]{2,1,0:T(8,128)(2,1)S(1)}, bf16[2,208,128]{2,1,0:T(8,128)(2,1)S(1)}, u32[]{:S(2)}, u32[]{:S(2)}) collective-permute-start(bf16[2,208,128]{2,1,0:T(8,128)(2,1)S(1)} %get-tuple-element.29), channel_id=1, source_target_pairs={{0,96},{16,112},{32,0},{48,16},{64,32},{80,48},{96,64},{112,80},{1... | collective-permute-start | bytes 319496 | tf_op jit(solution)/shard_map/ppermute | solution.py:302
  91.0 6.9 %collective-permute-start.7 = (bf16[2,208,128]{2,1,0:T(8,128)(2,1)S(1)}, bf16[2,208,128]{2,1,0:T(8,128)(2,1)S(1)}, u32[]{:S(2)}, u32[]{:S(2)}) collective-permute-start(bf16[2,208,128]{2,1,0:T(8,128)(2,1)S(1)} %get-tuple-element.30), channel_id=1, source_target_pairs={{0,64},{16,80},{32,96},{48,112},{64,0},{80,16},{96,32},{112,48},{1... | collective-permute-start | bytes 319496 | tf_op jit(solution)/shard_map/ppermute | solution.py:302
  98.0 6.5 %collective-permute-start.9 = (bf16[208,128]{1,0:T(8,128)(2,1)S(1)}, bf16[208,128]{1,0:T(8,128)(2,1)S(1)}, u32[]{:S(2)}, u32[]{:S(2)}) collective-permute-start(bf16[208,128]{1,0:T(8,128)(2,1)S(1)} %fusion.2), channel_id=1, source_target_pairs={{0,128},{16,144},{32,160},{48,176},{64,192},{80,208},{96,224},{112... | collective-permute-start | bytes 159752 | tf_op jit(solution)/shard_map/ppermute | solution.py:303
  111.1 0.9 copy-start.9

commit v4 on v3

--- a/solution.py
+++ b/solution.py
@@ -22,7 +22,8 @@
 
 NT = (((1,), (1,)), ((), ()))
 TN = (((0,), (0,)), ((), ()))
-COUNT_VMEM = 32 * 1024 * 1024
+COUNT_VMEM = 56 * 1024 * 1024
+UPDATE_VMEM = 8 * 1024 * 1024
 GRADIENT_VMEM = 48 * 1024 * 1024
 
 
@@ -274,6 +275,7 @@
     new_table, new_state = pl.pallas_call(
         update_kernel,
         out_shape=[jax.ShapeDtypeStruct(table.shape, jnp.float32), jax.ShapeDtypeStruct((1, rows), jnp.float32)],
+        compiler_params=pltpu.CompilerParams(vmem_limit_bytes=UPDATE_VMEM),
         cost_estimate=pl.CostEstimate(flops=1 << 20, bytes_accessed=2 << 20, transcendentals=0),
         name="row_adagrad",
     )(parts, table, state.reshape(1, rows))
@@ -288,10 +290,13 @@
     return [(i, (i & 9) | ((((i >> 1) + k) & 3) << 1)) for i in range(16)]
 
 
-def gather_src(lines):
+def gather_src(lines, beside, operands):
     near = jnp.stack([lines, lax.ppermute(lines, "src", HALVES)])
+    near, operands = lax.optimization_barrier((near, operands))
+    results = beside(*operands)
     own = jnp.concatenate([near] + [lax.ppermute(near, "src", x_step(k)) for k in (1, 2, 3)])
-    return own, lax.ppermute(own, "src", CORES)
+    own, results = lax.optimization_barrier((own, results))
+    return own, lax.ppermute(own, "src", CORES), results
 
 
 def scatter_src(own, other):
@@ -319,15 +324,15 @@
     member = lax.axis_index("src").reshape(1)
     source_blocks, target_lines = pack_tables(source_table, target_table)
     sources_all = lax.all_to_all(source_blocks, "dst", 0, 0)
-    targets_own, targets_other = gather_src(target_lines)
     slots = (1, BATCHES * BATCH)
-    n, m = counts(
+    lists = (
         batch_relation.reshape(BATCHES),
         edge_counts.reshape(1),
         edge_source.reshape(slots),
         edge_target.reshape(slots),
         negatives.reshape(slots),
     )
+    targets_own, targets_other, (n, m) = gather_src(target_lines, counts, lists)
     source_grad, own, other = gradients(member, sources_all, targets_own, targets_other, relations, n, m)
     source_parts = lax.all_to_all(source_grad, "dst", 0, 0)
     target_parts = scatter_src(own, other)

time: 116 us -> 98.6 us (0.85); the launches traced: 114 us -> 98.2 us
  local copies, waits for them, and re-layouts: 13 us -> 1.49 us
  starting transfers between devices: 33.7 us -> 30.4 us
    unnamed x24 -> x10, local copies, waits for them, and re-layouts: 13 us -> 1.45 us
    ppermute x3, waiting for transfers between devices: 3.15 us -> 0.01 us  [gather_src(): lax.ppermute(near, 'src', x_step(k))]
    all_to_all x1, waiting for transfers between devices: 3.86 us -> 6.89 us  [per_device(): source_parts = lax.all_to_all(source_grad, 'dst', 0, 0)]
    ppermute x1, waiting for transfers between devices: 2.45 us -> 0.01 us  [gather_src(): near = jnp.stack([lines, lax.ppermute(lines, 'src', HALVES)])]
    pallas_call x2, Pallas kernels: 4.35 us -> 2.12 us  [update(): pl.pallas_call(update_kernel, out_shape=[jax.ShapeDtypeStruct(table.shape...]
    ppermute x1, waiting for transfers between devices: 0.01 us -> 1.75 us  [gather_src(): return (own, lax.ppermute(own, 'src', CORES), results)]
    ppermute x3, starting transfers between devices: 4.87 us -> 3.5 us  [scatter_src(): lax.ppermute(sent[2 * k:2 * k + 2], 'src', x_step(k)).astype(jnp.float32)]
    pallas_call x1, Pallas kernels: 17.4 us -> 18.6 us  [counts(): pl.pallas_call(count_kernel, grid=(PART // COUNT_TILE,), in_specs=[smem,...]
  transfers between devices with their start and end apart: 12 -> 12, of which waited for: 7 -> 5; matrix products, arithmetic and copies ran while one was open for 2% -> 1% of each run, Pallas kernels for 17% -> 20%
where the time goes in v4:
time: 98.6 us; the launch traced here: 98.2 us
  Pallas kernels  45.1 us (46%)
  starting transfers between devices  30.4 us (31%)
  waiting for transfers between devices  18.6 us (19%)
  local copies, waits for them, and re-layouts  1.49 us (2%)
  between operations  1.43 us (1%)
  other arithmetic  1.08 us (1%)
    pallas_call x1, Pallas kernels, gradients(): pl.pallas_call(gradient_kernel, grid=(NREL + 1, PART // TILE), in_specs=[...  22.4 us
    pallas_call x1, Pallas kernels, counts(): pl.pallas_call(count_kernel, grid=(PART // COUNT_TILE,), in_specs=[smem,...  18.6 us
    all_to_all x1, starting transfers between devices, per_device(): sources_all = lax.all_to_all(source_blocks, 'dst', 0, 0)  8.68 us
    all_to_all x1, starting transfers between devices, per_device(): source_parts = lax.all_to_all(source_grad, 'dst', 0, 0)  8.12 us
    all_to_all x1, waiting for transfers between devices, per_device(): source_parts = lax.all_to_all(source_grad, 'dst', 0, 0)  6.89 us
    ppermute x3, waiting for transfers between devices, scatter_src(): lax.ppermute(sent[2 * k:2 * k + 2], 'src', x_step(k)).astype(jnp.float32)  5.01 us
    ppermute x1, waiting for transfers between devices, scatter_src(): far = lax.ppermute(here[1].astype(jnp.bfloat16), 'src', HALVES)  4.97 us
    ppermute x3, starting transfers between devices, gather_src(): lax.ppermute(near, 'src', x_step(k))  4.83 us
  transfers between devices with their start and end apart: 12, of which 5 were waited for; matrix products, arithmetic and copies ran while one was open for 1% of the time, Pallas kernels for 20%

profile of v4, /device:TPU:2, one launch (start us, length us, event | category | flops | bytes accessed | tf_op | source)
XLA Modules:
  0.0 98.2 jit_solution(1268229947042141049)
XLA Ops:
  0.6 2.0 %pack_tables.1 = (bf16[16,208,128]{2,1,0:T(8,128)(2,1)}, bf16[208,128]{1,0:T(8,128)(2,1)}) custom-call(f32[64,400]{1,0:T(8,128)} %table_ref.2, f32[64,400]{1,0:T(8,128)} %table_ref.3), custom_call_target="tpu_custom_call" | custom-call | tf_op jit(solution)/shard_map/pack_tables/pallas_call | solution.py:128
  2.6 3.2 %collective-permute-start = (bf16[208,128]{1,0:T(8,128)(2,1)}, bf16[208,128]{1,0:T(8,128)(2,1)S(1)}, u32[]{:S(2)}, u32[]{:S(2)}) collective-permute-start(bf16[208,128]{1,0:T(8,128)(2,1)} %get-tuple-element.25), channel_id=1, source_target_pairs={{0,128},{16,144},{32,160},{48,176},{64,192},{80,208},{96,224},{112... | collective-permute-start | bytes 159752 | tf_op jit(solution)/shard_map/ppermute | solution.py:294
  5.8 8.7 %all-to-all-start = ((bf16[16,208,128]{2,1,0:T(8,128)(2,1)}), bf16[16,208,128]{2,1,0:T(8,128)(2,1)S(1)}, u32[]{:S(2)}, u32[]{:S(2)}) async-start(bf16[16,208,128]{2,1,0:T(8,128)(2,1)} %get-tuple-element.24), calls=%async_computation | async-start | bytes 1703936 | tf_op jit(solution)/shard_map/all_to_all | solution.py:326
  15.1 0.0 collective-permute-done
  15.2 0.8 pad_maximum_fusion.2
  16.0 0.6 collective-permute-start.3
  16.6 2.4 %collective-permute-start.2 = (bf16[2,208,128]{2,1,0:T(8,128)(2,1)S(1)}, bf16[2,208,128]{2,1,0:T(8,128)(2,1)S(1)}, u32[]{:S(2)}, u32[]{:S(2)}) collective-permute-start(bf16[2,208,128]{2,1,0:T(8,128)(2,1)S(1)} %pad_maximum_fusion.2), channel_id=1, source_target_pairs={{0,64},{16,80},{32,96},{48,112},{64,0},{80,16},{96,32},{112,48},{1... | collective-permute-start | bytes 319496 | tf_op jit(solution)/shard_map/ppermute | solution.py:297
  19.0 1.8 %collective-permute-start.1 = (bf16[2,208,128]{2,1,0:T(8,128)(2,1)S(1)}, bf16[2,208,128]{2,1,0:T(8,128)(2,1)S(1)}, u32[]{:S(2)}, u32[]{:S(2)}) collective-permute-start(bf16[2,208,128]{2,1,0:T(8,128)(2,1)S(1)} %pad_maximum_fusion.2), channel_id=1, source_target_pairs={{0,32},{16,48},{32,64},{48,80},{64,96},{80,112},{96,0},{112,16},{1... | collective-permute-start | bytes 319496 | tf_op jit(solution)/shard_map/ppermute | solution.py:297
  20.8 18.6 %pair_counts.1 = (bf16[4,1024,1024]{2,1,0:T(8,128)(2,1)}, bf16[4,1024,1024]{2,1,0:T(8,128)(2,1)}) custom-call(s32[12]{0:T(128)} %bitcast.25, s32[1]{0:T(128)} %bitcast.17.cnt_ref, s32[1,6144]{1,0:T(1,128)} %bitcast.22, s32[1,6144]{1,0:T(1,128)} %bitcast.23, s32[1,6144]{1,0:T(1,128)} %bitcast.24), custom_call_target="tpu_custom_call" | custom-call | flops 12884901888 | bytes 16777216 | tf_op jit(solution)/shard_map/pair_counts/pallas_call | solution.py:88
  39.4 0.0 collective-permute-done.3
  39.4 0.0 collective-permute-done.2
  39.4 0.0 collective-permute-done.1
  39.4 0.1 pad_maximum_fusion.t_own_ref
  39.5 0.1 collective-permute-start.4
  39.6 1.8 %collective-permute-done.4.t_other_ref = bf16[8,208,128]{2,1,0:T(8,128)(2,1)S(1)} collective-permute-done((bf16[8,208,128]{2,1,0:T(8,128)(2,1)S(1)}, bf16[8,208,128]{2,1,0:T(8,128)(2,1)S(1)}, u32[]{:S(2)}, u32[]{:S(2)}) %collective-permute-start.4) | collective-permute-done | bytes 426016 | tf_op jit(solution)/shard_map/ppermute | solution.py:299
  41.4 0.0 all-to-all-done.s_ref
  41.4 0.0 copy-start.4
  41.4 1.4 %copy-done.4 = bf16[4,400,400]{2,1,0:T(8,128)(2,1)S(1)} copy-done((bf16[4,400,400]{2,1,0:T(8,128)(2,1)S(1)}, bf16[4,400,400]{2,1,0:T(8,128)(2,1)}, u32[]{:S(2)}) %copy-start.4) | copy-done | bytes 1280024
  42.8 0.0 copy-start.1
  42.8 0.0 copy-start.3
  42.8 0.0 copy-start
  42.8 0.0 copy-start.2
  42.8 22.4 %gradients.1 = (bf16[16,208,128]{2,1,0:T(8,128)(2,1)}, bf16[8,208,128]{2,1,0:T(8,128)(2,1)S(1)}, bf16[8,208,128]{2,1,0:T(8,128)(2,1)S(1)}) custom-call(s32[1]{0:T(128)} %bitcast.member_ref, bf16[16,208,128]{2,1,0:T(8,128)(2,1)S(1)} %all-to-all-done.s_ref, bf16[8,208,128]{2,1,0:T(8,128)(2,1)S(1)} %pad_maximum_fusion.t_own_ref, ...), custom_call_target="tpu_custom_call" | custom-call | flops 17179869184 | bytes 20971520 | tf_op jit(solution)/shard_map/gradients/pallas_call | solution.py:224
  65.2 0.1 collective-permute-start.5
  65.3 8.1 %all-to-all-start.1 = ((bf16[16,208,128]{2,1,0:T(8,128)(2,1)}), bf16[16,208,128]{2,1,0:T(8,128)(2,1)S(1)}, u32[]{:S(2)}, u32[]{:S(2)}) async-start(bf16[16,208,128]{2,1,0:T(8,128)(2,1)} %get-tuple-element.37), calls=%async_computation.1 | async-start | bytes 1703936 | tf_op jit(solution)/shard_map/all_to_all | solution.py:337
  73.4 0.0 collective-permute-done.5
  73.4 0.1 fusion.3
  73.6 0.1 collective-permute-start.6
  73.7 2.0 %collective-permute-start.8 = (bf16[2,208,128]{2,1,0:T(8,128)(2,1)S(1)}, bf16[2,208,128]{2,1,0:T(8,128)(2,1)S(1)}, u32[]{:S(2)}, u32[]{:S(2)}) collective-permute-start(bf16[2,208,128]{2,1,0:T(8,128)(2,1)S(1)} %get-tuple-element.47), channel_id=1, source_target_pairs={{0,96},{16,112},{32,0},{48,16},{64,32},{80,48},{96,64},{112,80},{1... | collective-permute-start | bytes 319496 | tf_op jit(solution)/shard_map/ppermute | solution.py:307
  75.7 1.4 %collective-permute-start.7 = (bf16[2,208,128]{2,1,0:T(8,128)(2,1)S(1)}, bf16[2,208,128]{2,1,0:T(8,128)(2,1)S(1)}, u32[]{:S(2)}, u32[]{:S(2)}) collective-permute-start(bf16[2,208,128]{2,1,0:T(8,128)(2,1)S(1)} %get-tuple-element.48), channel_id=1, source_target_pairs={{0,64},{16,80},{32,96},{48,112},{64,0},{80,16},{96,32},{112,48},{1... | collective-permute-start | bytes 319496 | tf_op jit(solution)/shard_map/ppermute | solution.py:307
  77.1 2.0 %collective-permute-done.6 = bf16[2,208,128]{2,1,0:T(8,128)(2,1)S(1)} collective-permute-done((bf16[2,208,128]{2,1,0:T(8,128)(2,1)S(1)}, bf16[2,208,128]{2,1,0:T(8,128)(2,1)S(1)}, u32[]{:S(2)}, u32[]{:S(2)}) %collective-permute-start.6) | collective-permute-done | bytes 106528 | tf_op jit(solution)/shard_map/ppermute | solution.py:307
  79.1 0.0 collective-permute-done.8
  79.1 3.0 %collective-permute-done.7 = bf16[2,208,128]{2,1,0:T(8,128)(2,1)S(1)} collective-permute-done((bf16[2,208,128]{2,1,0:T(8,128)(2,1)S(1)}, bf16[2,208,128]{2,1,0:T(8,128)(2,1)S(1)}, u32[]{:S(2)}, u32[]{:S(2)}) %collective-permute-start.7) | collective-permute-done | bytes 106528 | tf_op jit(solution)/shard_map/ppermute | solution.py:307
  82.1 0.1 fusion.1
  82.2 1.9 %collective-permute-start.9 = (bf16[208,128]{1,0:T(8,128)(2,1)S(1)}, bf16[208,128]{1,0:T(8,128)(2,1)S(1)}, u32[]{:S(2)}, u32[]{:S(2)}) collective-permute-start(bf16[208,128]{1,0:T(8,128)(2,1)S(1)} %fusion.2), channel_id=1, source_target_pairs={{0,128},{16,144},{32,160},{48,176},{64,192},{80,208},{96,224},{112... | collective-permute-start | bytes 159752 | tf_op jit(solution)/shard_map/ppermute | solution.py:308
  84.1 5.0 %collective-permute-done.9 = bf16[208,128]{1,0:T(8,128)(2,1)S(1)} collective-permute-done((bf16[208,128]{1,0:T(8,128)(2,1)S(1)}, bf16[208,128]{1,0:T(8,128)(2,1)S(1)}, u32[]{:S(2)}, u32[]{:S(2)}) %collective-permute-start.9) | collective-permute-done | bytes 53280 | tf_op jit(solution)/shard_map/ppermute | solution.py:308
  89.1 0.0 copy-done.1
  89.1 0.0 copy-done.3
  89.1 1.0 %row_adagrad.3 = (f32[64,400]{1,0:T(8,128)}, f32[1,64]{1,0:T(1,128)}) custom-call(f32[2,208,128]{2,1,0:T(8,128)S(1)} %pad_maximum_fusion.1.part_ref, f32[64,400]{1,0:T(8,128)S(1)} %copy-done.1, f32[1,64]{1,0:T(1,128)S(1)} %bitcast.19), custom_call_target="tpu_custom_call" | custom-call | flops 1048576 | bytes 2097152 | tf_op jit(solution)/shard_map/row_adagrad/pallas_call | solution.py:275
  90.2 6.9 %all-to-all-done.1.part_ref = bf16[16,208,128]{2,1,0:T(8,128)(2,1)S(1)} async-done(((bf16[16,208,128]{2,1,0:T(8,128)(2,1)}), bf16[16,208,128]{2,1,0:T(8,128)(2,1)S(1)}, u32[]{:S(2)}, u32[]{:S(2)}) %all-to-all-start.1) | async-done | bytes 852000 | tf_op jit(solution)/shard_map/all_to_all | solution.py:337
  97.1 0.0 copy-done
  97.1 0.0 copy-done.2
  97.1 1.1 %row_adagrad.2 = (f32[64,400]{1,0:T(8,128)}, f32[1,64]{1,0:T(1,128)}) custom-call(bf16[16,208,128]{2,1,0:T(8,128)(2,1)S(1)} %all-to-all-done.1.part_ref, f32[64,400]{1,0:T(8,128)S(1)} %copy-done, f32[1,64]{1,0:T(1,128)S(1)} %bitcast.18), custom_call_target="tpu_custom_call" | custom-call | flops 1048576 | bytes 2097152 | tf_op jit(solution)/shard_map/row_adagrad/pallas_call | solution.py:275
  (5 shorter events, 0.1 us)
Async XLA Ops:
  2.6 12.5 %collective-permute-start = (bf16[208,128]{1,0:T(8,128)(2,1)}, bf16[208,128]{1,0:T(8,128)(2,1)S(1)}, u32[]{:S(2)}, u32[]{:S(2)}) collective-permute-start(bf16[208,128]{1,0:T(8,128)(2,1)} %get-tuple-element.25), channel_id=1, source_target_pairs={{0,128},{16,144},{32,160},{48,176},{64,192},{80,208},{96,224},{112... | collective-permute-start | bytes 159752 | tf_op jit(solution)/shard_map/ppermute | solution.py:294
  5.8 35.6 %all-to-all-start = ((bf16[16,208,128]{2,1,0:T(8,128)(2,1)}), bf16[16,208,128]{2,1,0:T(8,128)(2,1)S(1)}, u32[]{:S(2)}, u32[]{:S(2)}) async-start(bf16[16,208,128]{2,1,0:T(8,128)(2,1)} %get-tuple-element.24), calls=%async_computation | async-start | bytes 1703936 | tf_op jit(solution)/shard_map/all_to_all | solution.py:326
  16.0 23.4 %collective-permute-start.3 = (bf16[2,208,128]{2,1,0:T(8,128)(2,1)S(1)}, bf16[2,208,128]{2,1,0:T(8,128)(2,1)S(1)}, u32[]{:S(2)}, u32[]{:S(2)}) collective-permute-start(bf16[2,208,128]{2,1,0:T(8,128)(2,1)S(1)} %pad_maximum_fusion.2), channel_id=1, source_target_pairs={{0,96},{16,112},{32,0},{48,16},{64,32},{80,48},{96,64},{112,80},{1... | collective-permute-start | bytes 319496 | tf_op jit(solution)/shard_map/ppermute | solution.py:297
  16.6 22.8 %collective-permute-start.2 = (bf16[2,208,128]{2,1,0:T(8,128)(2,1)S(1)}, bf16[2,208,128]{2,1,0:T(8,128)(2,1)S(1)}, u32[]{:S(2)}, u32[]{:S(2)}) collective-permute-start(bf16[2,208,128]{2,1,0:T(8,128)(2,1)S(1)} %pad_maximum_fusion.2), channel_id=1, source_target_pairs={{0,64},{16,80},{32,96},{48,112},{64,0},{80,16},{96,32},{112,48},{1... | collective-permute-start | bytes 319496 | tf_op jit(solution)/shard_map/ppermute | solution.py:297
  19.0 20.4 %collective-permute-start.1 = (bf16[2,208,128]{2,1,0:T(8,128)(2,1)S(1)}, bf16[2,208,128]{2,1,0:T(8,128)(2,1)S(1)}, u32[]{:S(2)}, u32[]{:S(2)}) collective-permute-start(bf16[2,208,128]{2,1,0:T(8,128)(2,1)S(1)} %pad_maximum_fusion.2), channel_id=1, source_target_pairs={{0,32},{16,48},{32,64},{48,80},{64,96},{80,112},{96,0},{112,16},{1... | collective-permute-start | bytes 319496 | tf_op jit(solution)/shard_map/ppermute | solution.py:297
  39.5 1.9 %collective-permute-start.4 = (bf16[8,208,128]{2,1,0:T(8,128)(2,1)S(1)}, bf16[8,208,128]{2,1,0:T(8,128)(2,1)S(1)}, u32[]{:S(2)}, u32[]{:S(2)}) collective-permute-start(bf16[8,208,128]{2,1,0:T(8,128)(2,1)S(1)} %pad_maximum_fusion.t_own_ref), channel_id=1, source_target_pairs={{0,16},{16,0},{32,48},{48,32},{64,80},{80,64},{96,112},{112,96},{1... | collective-permute-start | bytes 1277960 | tf_op jit(solution)/shard_map/ppermute | solution.py:299
  41.4 1.4 %copy-start.4 = (bf16[4,400,400]{2,1,0:T(8,128)(2,1)S(1)}, bf16[4,400,400]{2,1,0:T(8,128)(2,1)}, u32[]{:S(2)}) copy-start(bf16[4,400,400]{2,1,0:T(8,128)(2,1)} %rel_ref.1) | copy-start | bytes 3840004
  42.8 46.3 %copy-start.1 = (f32[64,400]{1,0:T(8,128)S(1)}, f32[64,400]{1,0:T(8,128)}, u32[]{:S(2)}) copy-start(f32[64,400]{1,0:T(8,128)} %table_ref.3) | copy-start | bytes 307204
  42.8 46.3 %copy-start.3 = (f32[64]{0:T(128)S(1)}, f32[64]{0:T(128)}, u32[]{:S(2)}) copy-start(f32[64]{0:T(128)} %param.13) | copy-start | bytes 772
  42.8 54.3 %copy-start = (f32[64,400]{1,0:T(8,128)S(1)}, f32[64,400]{1,0:T(8,128)}, u32[]{:S(2)}) copy-start(f32[64,400]{1,0:T(8,128)} %table_ref.2) | copy-start | bytes 307204
  42.8 54.3 %copy-start.2 = (f32[64]{0:T(128)S(1)}, f32[64]{0:T(128)}, u32[]{:S(2)}) copy-start(f32[64]{0:T(128)} %param.11) | copy-start | bytes 772
  65.2 8.2 %collective-permute-start.5 = (bf16[8,208,128]{2,1,0:T(8,128)(2,1)S(1)}, bf16[8,208,128]{2,1,0:T(8,128)(2,1)S(1)}, u32[]{:S(2)}, u32[]{:S(2)}) collective-permute-start(bf16[8,208,128]{2,1,0:T(8,128)(2,1)S(1)} %get-tuple-element.41), channel_id=1, source_target_pairs={{0,16},{16,0},{32,48},{48,32},{64,80},{80,64},{96,112},{112,96},{1... | collective-permute-start | bytes 1277960 | tf_op jit(solution)/shard_map/ppermute | solution.py:303
  65.3 31.8 %all-to-all-start.1 = ((bf16[16,208,128]{2,1,0:T(8,128)(2,1)}), bf16[16,208,128]{2,1,0:T(8,128)(2,1)S(1)}, u32[]{:S(2)}, u32[]{:S(2)}) async-start(bf16[16,208,128]{2,1,0:T(8,128)(2,1)} %get-tuple-element.37), calls=%async_computation.1 | async-start | bytes 1703936 | tf_op jit(solution)/shard_map/all_to_all | solution.py:337
  73.6 5.5 %collective-permute-start.6 = (bf16[2,208,128]{2,1,0:T(8,128)(2,1)S(1)}, bf16[2,208,128]{2,1,0:T(8,128)(2,1)S(1)}, u32[]{:S(2)}, u32[]{:S(2)}) collective-permute-start(bf16[2,208,128]{2,1,0:T(8,128)(2,1)S(1)} %get-tuple-element.46), channel_id=1, source_target_pairs={{0,32},{16,48},{32,64},{48,80},{64,96},{80,112},{96,0},{112,16},{1... | collective-permute-start | bytes 319496 | tf_op jit(solution)/shard_map/ppermute | solution.py:307
  73.7 5.4 %collective-permute-start.8 = (bf16[2,208,128]{2,1,0:T(8,128)(2,1)S(1)}, bf16[2,208,128]{2,1,0:T(8,128)(2,1)S(1)}, u32[]{:S(2)}, u32[]{:S(2)}) collective-permute-start(bf16[2,208,128]{2,1,0:T(8,128)(2,1)S(1)} %get-tuple-element.47), channel_id=1, source_target_pairs={{0,96},{16,112},{32,0},{48,16},{64,32},{80,48},{96,64},{112,80},{1... | collective-permute-start | bytes 319496 | tf_op jit(solution)/shard_map/ppermute | solution.py:307
  75.7 6.4 %collective-permute-start.7 = (bf16[2,208,128]{2,1,0:T(8,128)(2,1)S(1)}, bf16[2,208,128]{2,1,0:T(8,128)(2,1)S(1)}, u32[]{:S(2)}, u32[]{:S(2)}) collective-permute-start(bf16[2,208,128]{2,1,0:T(8,128)(2,1)S(1)} %get-tuple-element.48), channel_id=1, source_target_pairs={{0,64},{16,80},{32,96},{48,112},{64,0},{80,16},{96,32},{112,48},{1... | collective-permute-start | bytes 319496 | tf_op jit(solution)/shard_map/ppermute | solution.py:307
  82.2 6.9 %collective-permute-start.9 = (bf16[208,128]{1,0:T(8,128)(2,1)S(1)}, bf16[208,128]{1,0:T(8,128)(2,1)S(1)}, u32[]{:S(2)}, u32[]{:S(2)}) collective-permute-start(bf16[208,128]{1,0:T(8,128)(2,1)S(1)} %fusion.2), channel_id=1, source_target_pairs={{0,128},{16,144},{32,160},{48,176},{64,192},{80,208},{96,224},{112... | collective-permute-start | bytes 159752 | tf_op jit(solution)/shard_map/ppermute | solution.py:308

commit v5 on v4

--- a/solution.py
+++ b/solution.py
@@ -63,10 +63,22 @@
         srch[BATCHES:] = jnp.zeros((16 - BATCHES, PART), jnp.float32)
         negh[BATCHES:] = jnp.zeros((16 - BATCHES, PART), jnp.float32)
 
-    acc[...] = jnp.zeros_like(acc)
+    for r in range(NREL):
+        uses = jnp.int32(0)
+        for b in range(BATCHES):
+            uses = uses + (rel_ref[b] == r).astype(jnp.int32)
+
+        @pl.when(uses == 0)
+        def _():
+            acc[r] = jnp.zeros((COUNT_TILE, PART), jnp.float32)
+
     for b in range(BATCHES):
         oht = one_hot_columns(et_ref[:, b * BATCH : (b + 1) * BATCH], COUNT_TILE, step * COUNT_TILE, 0.5, ONE_HOT)
-        acc[rel_ref[b]] += dot(oht, ohs[b])
+        r = rel_ref[b]
+        seen = jnp.int32(0)
+        for c in range(b):
+            seen = seen + (rel_ref[c] == r).astype(jnp.int32)
+        acc[r] = jnp.where(seen > 0, acc[r], 0.0) + dot(oht, ohs[b])
 
     n_ref[...] = acc[...].astype(jnp.bfloat16)
     lanes = pl.ds(pl.multiple_of(step * COUNT_TILE, COUNT_TILE), COUNT_TILE)

time: 98.6 us -> 99.3 us (level)
  transfers between devices with their start and end apart: 12 -> 12, of which waited for: 5 -> 5; matrix products, arithmetic and copies ran while one was open for 1% -> 1% of each run, Pallas kernels for 20% -> 21%
where the time goes in v5:
time: 99.3 us; the launch traced here: 98.8 us
  Pallas kernels  45.8 us (46%)
  starting transfers between devices  30.4 us (31%)
  waiting for transfers between devices  18.6 us (19%)
  local copies, waits for them, and re-layouts  1.49 us (2%)
  between operations  1.43 us (1%)
  other arithmetic  1.08 us (1%)
    pallas_call x1, Pallas kernels, gradients(): pl.pallas_call(gradient_kernel, grid=(NREL + 1, PART // TILE), in_specs=[...  22.4 us
    pallas_call x1, Pallas kernels, counts(): pl.pallas_call(count_kernel, grid=(PART // COUNT_TILE,), in_specs=[smem,...  19.3 us
    all_to_all x1, starting transfers between devices, per_device(): sources_all = lax.all_to_all(source_blocks, 'dst', 0, 0)  8.68 us
    all_to_all x1, starting transfers between devices, per_device(): source_parts = lax.all_to_all(source_grad, 'dst', 0, 0)  8.12 us
    all_to_all x1, waiting for transfers between devices, per_device(): source_parts = lax.all_to_all(source_grad, 'dst', 0, 0)  6.88 us
    ppermute x3, waiting for transfers between devices, scatter_src(): lax.ppermute(sent[2 * k:2 * k + 2], 'src', x_step(k)).astype(jnp.float32)  5.01 us
    ppermute x1, waiting for transfers between devices, scatter_src(): far = lax.ppermute(here[1].astype(jnp.bfloat16), 'src', HALVES)  4.98 us
    ppermute x3, starting transfers between devices, gather_src(): lax.ppermute(near, 'src', x_step(k))  4.83 us
  transfers between devices with their start and end apart: 12, of which 5 were waited for; matrix products, arithmetic and copies ran while one was open for 1% of the time, Pallas kernels for 21%

profile of v5, /device:TPU:2, one launch (start us, length us, event | category | flops | bytes accessed | tf_op | source)
XLA Modules:
  0.0 98.8 jit_solution(15526753062875579627)
XLA Ops:
  0.6 2.0 %pack_tables.1 = (bf16[16,208,128]{2,1,0:T(8,128)(2,1)}, bf16[208,128]{1,0:T(8,128)(2,1)}) custom-call(f32[64,400]{1,0:T(8,128)} %table_ref.2, f32[64,400]{1,0:T(8,128)} %table_ref.3), custom_call_target="tpu_custom_call" | custom-call | tf_op jit(solution)/shard_map/pack_tables/pallas_call | solution.py:140
  2.6 3.2 %collective-permute-start = (bf16[208,128]{1,0:T(8,128)(2,1)}, bf16[208,128]{1,0:T(8,128)(2,1)S(1)}, u32[]{:S(2)}, u32[]{:S(2)}) collective-permute-start(bf16[208,128]{1,0:T(8,128)(2,1)} %get-tuple-element.25), channel_id=1, source_target_pairs={{0,128},{16,144},{32,160},{48,176},{64,192},{80,208},{96,224},{112... | collective-permute-start | bytes 159752 | tf_op jit(solution)/shard_map/ppermute | solution.py:306
  5.8 8.7 %all-to-all-start = ((bf16[16,208,128]{2,1,0:T(8,128)(2,1)}), bf16[16,208,128]{2,1,0:T(8,128)(2,1)S(1)}, u32[]{:S(2)}, u32[]{:S(2)}) async-start(bf16[16,208,128]{2,1,0:T(8,128)(2,1)} %get-tuple-element.24), calls=%async_computation | async-start | bytes 1703936 | tf_op jit(solution)/shard_map/all_to_all | solution.py:338
  15.1 0.0 collective-permute-done
  15.2 0.8 pad_maximum_fusion.2
  16.0 0.6 collective-permute-start.3
  16.6 2.4 %collective-permute-start.2 = (bf16[2,208,128]{2,1,0:T(8,128)(2,1)S(1)}, bf16[2,208,128]{2,1,0:T(8,128)(2,1)S(1)}, u32[]{:S(2)}, u32[]{:S(2)}) collective-permute-start(bf16[2,208,128]{2,1,0:T(8,128)(2,1)S(1)} %pad_maximum_fusion.2), channel_id=1, source_target_pairs={{0,64},{16,80},{32,96},{48,112},{64,0},{80,16},{96,32},{112,48},{1... | collective-permute-start | bytes 319496 | tf_op jit(solution)/shard_map/ppermute | solution.py:309
  19.0 1.8 %collective-permute-start.1 = (bf16[2,208,128]{2,1,0:T(8,128)(2,1)S(1)}, bf16[2,208,128]{2,1,0:T(8,128)(2,1)S(1)}, u32[]{:S(2)}, u32[]{:S(2)}) collective-permute-start(bf16[2,208,128]{2,1,0:T(8,128)(2,1)S(1)} %pad_maximum_fusion.2), channel_id=1, source_target_pairs={{0,32},{16,48},{32,64},{48,80},{64,96},{80,112},{96,0},{112,16},{1... | collective-permute-start | bytes 319496 | tf_op jit(solution)/shard_map/ppermute | solution.py:309
  20.8 19.3 %pair_counts.1 = (bf16[4,1024,1024]{2,1,0:T(8,128)(2,1)}, bf16[4,1024,1024]{2,1,0:T(8,128)(2,1)}) custom-call(s32[12]{0:T(128)} %bitcast.25, s32[1]{0:T(128)} %bitcast.17.cnt_ref, s32[1,6144]{1,0:T(1,128)} %bitcast.22, s32[1,6144]{1,0:T(1,128)} %bitcast.23, s32[1,6144]{1,0:T(1,128)} %bitcast.24), custom_call_target="tpu_custom_call" | custom-call | flops 12884901888 | bytes 16777216 | tf_op jit(solution)/shard_map/pair_counts/pallas_call | solution.py:100
  40.1 0.0 collective-permute-done.3
  40.1 0.0 collective-permute-done.2
  40.1 0.0 collective-permute-done.1
  40.1 0.1 pad_maximum_fusion.t_own_ref
  40.2 0.1 collective-permute-start.4
  40.3 1.8 %collective-permute-done.4.t_other_ref = bf16[8,208,128]{2,1,0:T(8,128)(2,1)S(1)} collective-permute-done((bf16[8,208,128]{2,1,0:T(8,128)(2,1)S(1)}, bf16[8,208,128]{2,1,0:T(8,128)(2,1)S(1)}, u32[]{:S(2)}, u32[]{:S(2)}) %collective-permute-start.4) | collective-permute-done | bytes 426016 | tf_op jit(solution)/shard_map/ppermute | solution.py:311
  42.0 0.0 all-to-all-done.s_ref
  42.0 0.0 copy-start.4
  42.0 1.4 %copy-done.4 = bf16[4,400,400]{2,1,0:T(8,128)(2,1)S(1)} copy-done((bf16[4,400,400]{2,1,0:T(8,128)(2,1)S(1)}, bf16[4,400,400]{2,1,0:T(8,128)(2,1)}, u32[]{:S(2)}) %copy-start.4) | copy-done | bytes 1280024
  43.5 0.0 copy-start.1
  43.5 0.0 copy-start.3
  43.5 0.0 copy-start
  43.5 0.0 copy-start.2
  43.5 22.4 %gradients.1 = (bf16[16,208,128]{2,1,0:T(8,128)(2,1)}, bf16[8,208,128]{2,1,0:T(8,128)(2,1)S(1)}, bf16[8,208,128]{2,1,0:T(8,128)(2,1)S(1)}) custom-call(s32[1]{0:T(128)} %bitcast.member_ref, bf16[16,208,128]{2,1,0:T(8,128)(2,1)S(1)} %all-to-all-done.s_ref, bf16[8,208,128]{2,1,0:T(8,128)(2,1)S(1)} %pad_maximum_fusion.t_own_ref, ...), custom_call_target="tpu_custom_call" | custom-call | flops 17179869184 | bytes 20971520 | tf_op jit(solution)/shard_map/gradients/pallas_call | solution.py:236
  65.9 0.1 collective-permute-start.5
  66.0 8.1 %all-to-all-start.1 = ((bf16[16,208,128]{2,1,0:T(8,128)(2,1)}), bf16[16,208,128]{2,1,0:T(8,128)(2,1)S(1)}, u32[]{:S(2)}, u32[]{:S(2)}) async-start(bf16[16,208,128]{2,1,0:T(8,128)(2,1)} %get-tuple-element.37), calls=%async_computation.1 | async-start | bytes 1703936 | tf_op jit(solution)/shard_map/all_to_all | solution.py:349
  74.1 0.0 collective-permute-done.5
  74.1 0.1 fusion.3
  74.3 0.1 collective-permute-start.6
  74.3 2.0 %collective-permute-start.8 = (bf16[2,208,128]{2,1,0:T(8,128)(2,1)S(1)}, bf16[2,208,128]{2,1,0:T(8,128)(2,1)S(1)}, u32[]{:S(2)}, u32[]{:S(2)}) collective-permute-start(bf16[2,208,128]{2,1,0:T(8,128)(2,1)S(1)} %get-tuple-element.47), channel_id=1, source_target_pairs={{0,96},{16,112},{32,0},{48,16},{64,32},{80,48},{96,64},{112,80},{1... | collective-permute-start | bytes 319496 | tf_op jit(solution)/shard_map/ppermute | solution.py:319
  76.4 1.4 %collective-permute-start.7 = (bf16[2,208,128]{2,1,0:T(8,128)(2,1)S(1)}, bf16[2,208,128]{2,1,0:T(8,128)(2,1)S(1)}, u32[]{:S(2)}, u32[]{:S(2)}) collective-permute-start(bf16[2,208,128]{2,1,0:T(8,128)(2,1)S(1)} %get-tuple-element.48), channel_id=1, source_target_pairs={{0,64},{16,80},{32,96},{48,112},{64,0},{80,16},{96,32},{112,48},{1... | collective-permute-start | bytes 319496 | tf_op jit(solution)/shard_map/ppermute | solution.py:319
  77.8 2.0 %collective-permute-done.6 = bf16[2,208,128]{2,1,0:T(8,128)(2,1)S(1)} collective-permute-done((bf16[2,208,128]{2,1,0:T(8,128)(2,1)S(1)}, bf16[2,208,128]{2,1,0:T(8,128)(2,1)S(1)}, u32[]{:S(2)}, u32[]{:S(2)}) %collective-permute-start.6) | collective-permute-done | bytes 106528 | tf_op jit(solution)/shard_map/ppermute | solution.py:319
  79.8 0.0 collective-permute-done.8
  79.8 3.0 %collective-permute-done.7 = bf16[2,208,128]{2,1,0:T(8,128)(2,1)S(1)} collective-permute-done((bf16[2,208,128]{2,1,0:T(8,128)(2,1)S(1)}, bf16[2,208,128]{2,1,0:T(8,128)(2,1)S(1)}, u32[]{:S(2)}, u32[]{:S(2)}) %collective-permute-start.7) | collective-permute-done | bytes 106528 | tf_op jit(solution)/shard_map/ppermute | solution.py:319
  82.8 0.1 fusion.1
  82.8 1.9 %collective-permute-start.9 = (bf16[208,128]{1,0:T(8,128)(2,1)S(1)}, bf16[208,128]{1,0:T(8,128)(2,1)S(1)}, u32[]{:S(2)}, u32[]{:S(2)}) collective-permute-start(bf16[208,128]{1,0:T(8,128)(2,1)S(1)} %fusion.2), channel_id=1, source_target_pairs={{0,128},{16,144},{32,160},{48,176},{64,192},{80,208},{96,224},{112... | collective-permute-start | bytes 159752 | tf_op jit(solution)/shard_map/ppermute | solution.py:320
  84.8 5.0 %collective-permute-done.9 = bf16[208,128]{1,0:T(8,128)(2,1)S(1)} collective-permute-done((bf16[208,128]{1,0:T(8,128)(2,1)S(1)}, bf16[208,128]{1,0:T(8,128)(2,1)S(1)}, u32[]{:S(2)}, u32[]{:S(2)}) %collective-permute-start.9) | collective-permute-done | bytes 53280 | tf_op jit(solution)/shard_map/ppermute | solution.py:320
  89.8 0.0 copy-done.1
  89.8 0.0 copy-done.3
  89.8 1.0 %row_adagrad.3 = (f32[64,400]{1,0:T(8,128)}, f32[1,64]{1,0:T(1,128)}) custom-call(f32[2,208,128]{2,1,0:T(8,128)S(1)} %pad_maximum_fusion.1.part_ref, f32[64,400]{1,0:T(8,128)S(1)} %copy-done.1, f32[1,64]{1,0:T(1,128)S(1)} %bitcast.19), custom_call_target="tpu_custom_call" | custom-call | flops 1048576 | bytes 2097152 | tf_op jit(solution)/shard_map/row_adagrad/pallas_call | solution.py:287
  90.9 6.9 %all-to-all-done.1.part_ref = bf16[16,208,128]{2,1,0:T(8,128)(2,1)S(1)} async-done(((bf16[16,208,128]{2,1,0:T(8,128)(2,1)}), bf16[16,208,128]{2,1,0:T(8,128)(2,1)S(1)}, u32[]{:S(2)}, u32[]{:S(2)}) %all-to-all-start.1) | async-done | bytes 852000 | tf_op jit(solution)/shard_map/all_to_all | solution.py:349
  97.8 0.0 copy-done
  97.8 0.0 copy-done.2
  97.8 1.1 %row_adagrad.2 = (f32[64,400]{1,0:T(8,128)}, f32[1,64]{1,0:T(1,128)}) custom-call(bf16[16,208,128]{2,1,0:T(8,128)(2,1)S(1)} %all-to-all-done.1.part_ref, f32[64,400]{1,0:T(8,128)S(1)} %copy-done, f32[1,64]{1,0:T(1,128)S(1)} %bitcast.18), custom_call_target="tpu_custom_call" | custom-call | flops 1048576 | bytes 2097152 | tf_op jit(solution)/shard_map/row_adagrad/pallas_call | solution.py:287
  (5 shorter events, 0.1 us)
Async XLA Ops:
  2.6 12.5 %collective-permute-start = (bf16[208,128]{1,0:T(8,128)(2,1)}, bf16[208,128]{1,0:T(8,128)(2,1)S(1)}, u32[]{:S(2)}, u32[]{:S(2)}) collective-permute-start(bf16[208,128]{1,0:T(8,128)(2,1)} %get-tuple-element.25), channel_id=1, source_target_pairs={{0,128},{16,144},{32,160},{48,176},{64,192},{80,208},{96,224},{112... | collective-permute-start | bytes 159752 | tf_op jit(solution)/shard_map/ppermute | solution.py:306
  5.8 36.2 %all-to-all-start = ((bf16[16,208,128]{2,1,0:T(8,128)(2,1)}), bf16[16,208,128]{2,1,0:T(8,128)(2,1)S(1)}, u32[]{:S(2)}, u32[]{:S(2)}) async-start(bf16[16,208,128]{2,1,0:T(8,128)(2,1)} %get-tuple-element.24), calls=%async_computation | async-start | bytes 1703936 | tf_op jit(solution)/shard_map/all_to_all | solution.py:338
  16.0 24.1 %collective-permute-start.3 = (bf16[2,208,128]{2,1,0:T(8,128)(2,1)S(1)}, bf16[2,208,128]{2,1,0:T(8,128)(2,1)S(1)}, u32[]{:S(2)}, u32[]{:S(2)}) collective-permute-start(bf16[2,208,128]{2,1,0:T(8,128)(2,1)S(1)} %pad_maximum_fusion.2), channel_id=1, source_target_pairs={{0,96},{16,112},{32,0},{48,16},{64,32},{80,48},{96,64},{112,80},{1... | collective-permute-start | bytes 319496 | tf_op jit(solution)/shard_map/ppermute | solution.py:309
  16.6 23.5 %collective-permute-start.2 = (bf16[2,208,128]{2,1,0:T(8,128)(2,1)S(1)}, bf16[2,208,128]{2,1,0:T(8,128)(2,1)S(1)}, u32[]{:S(2)}, u32[]{:S(2)}) collective-permute-start(bf16[2,208,128]{2,1,0:T(8,128)(2,1)S(1)} %pad_maximum_fusion.2), channel_id=1, source_target_pairs={{0,64},{16,80},{32,96},{48,112},{64,0},{80,16},{96,32},{112,48},{1... | collective-permute-start | bytes 319496 | tf_op jit(solution)/shard_map/ppermute | solution.py:309
  19.0 21.1 %collective-permute-start.1 = (bf16[2,208,128]{2,1,0:T(8,128)(2,1)S(1)}, bf16[2,208,128]{2,1,0:T(8,128)(2,1)S(1)}, u32[]{:S(2)}, u32[]{:S(2)}) collective-permute-start(bf16[2,208,128]{2,1,0:T(8,128)(2,1)S(1)} %pad_maximum_fusion.2), channel_id=1, source_target_pairs={{0,32},{16,48},{32,64},{48,80},{64,96},{80,112},{96,0},{112,16},{1... | collective-permute-start | bytes 319496 | tf_op jit(solution)/shard_map/ppermute | solution.py:309
  40.2 1.9 %collective-permute-start.4 = (bf16[8,208,128]{2,1,0:T(8,128)(2,1)S(1)}, bf16[8,208,128]{2,1,0:T(8,128)(2,1)S(1)}, u32[]{:S(2)}, u32[]{:S(2)}) collective-permute-start(bf16[8,208,128]{2,1,0:T(8,128)(2,1)S(1)} %pad_maximum_fusion.t_own_ref), channel_id=1, source_target_pairs={{0,16},{16,0},{32,48},{48,32},{64,80},{80,64},{96,112},{112,96},{1... | collective-permute-start | bytes 1277960 | tf_op jit(solution)/shard_map/ppermute | solution.py:311
  42.0 1.4 %copy-start.4 = (bf16[4,400,400]{2,1,0:T(8,128)(2,1)S(1)}, bf16[4,400,400]{2,1,0:T(8,128)(2,1)}, u32[]{:S(2)}) copy-start(bf16[4,400,400]{2,1,0:T(8,128)(2,1)} %rel_ref.1) | copy-start | bytes 3840004
  43.5 46.3 %copy-start.1 = (f32[64,400]{1,0:T(8,128)S(1)}, f32[64,400]{1,0:T(8,128)}, u32[]{:S(2)}) copy-start(f32[64,400]{1,0:T(8,128)} %table_ref.3) | copy-start | bytes 307204
  43.5 46.4 %copy-start.3 = (f32[64]{0:T(128)S(1)}, f32[64]{0:T(128)}, u32[]{:S(2)}) copy-start(f32[64]{0:T(128)} %param.13) | copy-start | bytes 772
  43.5 54.3 %copy-start = (f32[64,400]{1,0:T(8,128)S(1)}, f32[64,400]{1,0:T(8,128)}, u32[]{:S(2)}) copy-start(f32[64,400]{1,0:T(8,128)} %table_ref.2) | copy-start | bytes 307204
  43.5 54.3 %copy-start.2 = (f32[64]{0:T(128)S(1)}, f32[64]{0:T(128)}, u32[]{:S(2)}) copy-start(f32[64]{0:T(128)} %param.11) | copy-start | bytes 772
  65.9 8.2 %collective-permute-start.5 = (bf16[8,208,128]{2,1,0:T(8,128)(2,1)S(1)}, bf16[8,208,128]{2,1,0:T(8,128)(2,1)S(1)}, u32[]{:S(2)}, u32[]{:S(2)}) collective-permute-start(bf16[8,208,128]{2,1,0:T(8,128)(2,1)S(1)} %get-tuple-element.41), channel_id=1, source_target_pairs={{0,16},{16,0},{32,48},{48,32},{64,80},{80,64},{96,112},{112,96},{1... | collective-permute-start | bytes 1277960 | tf_op jit(solution)/shard_map/ppermute | solution.py:315
  66.0 31.8 %all-to-all-start.1 = ((bf16[16,208,128]{2,1,0:T(8,128)(2,1)}), bf16[16,208,128]{2,1,0:T(8,128)(2,1)S(1)}, u32[]{:S(2)}, u32[]{:S(2)}) async-start(bf16[16,208,128]{2,1,0:T(8,128)(2,1)} %get-tuple-element.37), calls=%async_computation.1 | async-start | bytes 1703936 | tf_op jit(solution)/shard_map/all_to_all | solution.py:349
  74.3 5.5 %collective-permute-start.6 = (bf16[2,208,128]{2,1,0:T(8,128)(2,1)S(1)}, bf16[2,208,128]{2,1,0:T(8,128)(2,1)S(1)}, u32[]{:S(2)}, u32[]{:S(2)}) collective-permute-start(bf16[2,208,128]{2,1,0:T(8,128)(2,1)S(1)} %get-tuple-element.46), channel_id=1, source_target_pairs={{0,32},{16,48},{32,64},{48,80},{64,96},{80,112},{96,0},{112,16},{1... | collective-permute-start | bytes 319496 | tf_op jit(solution)/shard_map/ppermute | solution.py:319
  74.3 5.4 %collective-permute-start.8 = (bf16[2,208,128]{2,1,0:T(8,128)(2,1)S(1)}, bf16[2,208,128]{2,1,0:T(8,128)(2,1)S(1)}, u32[]{:S(2)}, u32[]{:S(2)}) collective-permute-start(bf16[2,208,128]{2,1,0:T(8,128)(2,1)S(1)} %get-tuple-element.47), channel_id=1, source_target_pairs={{0,96},{16,112},{32,0},{48,16},{64,32},{80,48},{96,64},{112,80},{1... | collective-permute-start | bytes 319496 | tf_op jit(solution)/shard_map/ppermute | solution.py:319
  76.4 6.4 %collective-permute-start.7 = (bf16[2,208,128]{2,1,0:T(8,128)(2,1)S(1)}, bf16[2,208,128]{2,1,0:T(8,128)(2,1)S(1)}, u32[]{:S(2)}, u32[]{:S(2)}) collective-permute-start(bf16[2,208,128]{2,1,0:T(8,128)(2,1)S(1)} %get-tuple-element.48), channel_id=1, source_target_pairs={{0,64},{16,80},{32,96},{48,112},{64,0},{80,16},{96,32},{112,48},{1... | collective-permute-start | bytes 319496 | tf_op jit(solution)/shard_map/ppermute | solution.py:319
  82.8 6.9 %collective-permute-start.9 = (bf16[208,128]{1,0:T(8,128)(2,1)S(1)}, bf16[208,128]{1,0:T(8,128)(2,1)S(1)}, u32[]{:S(2)}, u32[]{:S(2)}) collective-permute-start(bf16[208,128]{1,0:T(8,128)(2,1)S(1)} %fusion.2), channel_id=1, source_target_pairs={{0,128},{16,144},{32,160},{48,176},{64,192},{80,208},{96,224},{112... | collective-permute-start | bytes 159752 | tf_op jit(solution)/shard_map/ppermute | solution.py:320
